TPU v7x, 128 devices: a whole 4x4x4 slice. The times are simulated.
128 devices in a mesh: gx: 4 (over z), gy: 32 (over y, x, core).
Axes of the slice: x: 4, y: 4, z: 4, core: 2. Of those that a mesh axis runs over, the one named last changes fastest.
Arguments:
- atm_fields: bfloat16 [4096, 512, 128], P(('gx', 'gy')), may hold values from -6 to 6
- neighbours: int32 [4096, 4], P(('gx', 'gy')), may hold values from 0 to 4095, as said below
- send_slots: int32 [128, 32, 2], P(('gx', 'gy')), may hold values from 0 to 31, as said below
- send_counts: int32 [128, 32], P(('gx', 'gy')), may hold values from 0 to 2, as said below
- tile_weights: bfloat16 [16384, 384, 128], P(('gx', 'gy')), may hold values from -0.109375 to 0.109375
- tile_rows: int32 [16384], P(('gx', 'gy')), may hold values from 0 to 7
- tile_cols: int32 [16384], P(('gx', 'gy')), may hold values from 0 to 63, as said below
Outputs:
- ocean_fields: bfloat16 [1024, 512, 128], P(('gx', 'gy'))
Inputs may be any that keep to these rules, and one draw needn't show every extreme that they name: `neighbours`: each neighbour lies within 8 blocks of its block along the curve, and that distance is reached. `send_slots`: the live slots of a device name distinct blocks of it; every block of a device is in exactly one live slot. `send_counts`: A device's counts sum to 32; every device fills all 2 slots to some owner. `tile_cols`: each of the 64 received slots of a device is named by exactly two of its tiles.
All inputs are finite; a program needn't handle non-finite values.
Results may differ from a plain program's by a relative error of at most 0.0041.
Values may be sent and summed in bfloat16 or wider, within the bound.
No kernel may reach another device: no remote copies, remote signals or barrier semaphores. Data moves between devices by JAX's collectives and lax.ppermute only.
A program may use at most 192 MiB of HBM per device.

v0:
```python
import jax
import jax.numpy as jnp
from jax import lax
from jax.sharding import PartitionSpec as P


def with_halo(block, sides, width):
    for axis, dim in sides:
        count = lax.axis_size(axis)
        forward = [(i, i + 1) for i in range(count - 1)]
        backward = [(target, source) for source, target in forward]
        low = lax.ppermute(
            lax.slice_in_dim(block, block.shape[dim] - width, None, axis=dim), axis, forward
        )
        high = lax.ppermute(lax.slice_in_dim(block, 0, width, axis=dim), axis, backward)
        block = jnp.concatenate([low, block, high], axis=dim)
    return block


def body(atm_fields, neighbours, send_slots, send_counts, tile_weights, tile_rows, tile_cols):
    block_count = atm_fields.shape[0]
    column_count = atm_fields.shape[1]
    cell_count = atm_fields.shape[2]
    peer_count = lax.axis_size("gy")
    capacity = send_slots.shape[2]
    halo_width = block_count // 4
    slot_order = send_slots.reshape(-1)
    planned = send_counts.reshape(peer_count, 1)
    extended = with_halo(atm_fields, ((("gx", "gy"), 0),), halo_width)
    first_index = lax.axis_index(("gx", "gy")) * block_count - halo_width
    local_index = neighbours - first_index
    east_side = extended[local_index[:, 0]].astype(jnp.float32)
    west_side = extended[local_index[:, 1]].astype(jnp.float32)
    north_side = extended[local_index[:, 2]].astype(jnp.float32)
    south_side = extended[local_index[:, 3]].astype(jnp.float32)
    grad_x = (0.5 * (east_side - west_side)).astype(jnp.bfloat16)
    grad_y = (0.5 * (north_side - south_side)).astype(jnp.bfloat16)
    payload = jnp.concatenate([atm_fields, jnp.concatenate([grad_x, grad_y], axis=2)], axis=2)
    outgoing = payload[slot_order].reshape(peer_count, capacity, column_count, 3 * cell_count)
    incoming, arrived = (
        lax.all_to_all(outgoing, "gy", split_axis=0, concat_axis=0, tiled=True),
        lax.all_to_all(planned, "gy", split_axis=0, concat_axis=0, tiled=True),
    )
    occupied = lax.broadcasted_iota(jnp.int32, (peer_count, capacity), 1) < arrived
    received = jnp.where(occupied[:, :, None, None], incoming, jnp.zeros_like(incoming))
    received = received.reshape(peer_count * capacity, column_count, 3 * cell_count)
    ocean_count = block_count // 4
    tile_count = tile_weights.shape[0]
    group_size = 16
    step_count = tile_count // group_size
    ocean_ids = lax.broadcasted_iota(jnp.int32, (ocean_count, group_size), 0)

    def add_group(total, group_index):
        start = group_index * group_size
        weights = lax.dynamic_slice_in_dim(tile_weights, start, group_size, 0)
        row_index = lax.dynamic_slice_in_dim(tile_rows, start, group_size, 0)
        column_index = lax.dynamic_slice_in_dim(tile_cols, start, group_size, 0)
        chosen = received[column_index]
        products = jnp.einsum("gcj,gjk->gck", chosen, weights, preferred_element_type=jnp.float32)
        selector = (row_index[None, :] == ocean_ids).astype(jnp.float32)
        total = total + jnp.einsum(
            "og,gck->ock", selector, products, precision=lax.Precision.HIGHEST
        )
        return (total, None)

    start_total = jnp.zeros((ocean_count, column_count, cell_count), jnp.float32)
    total, unused = lax.scan(add_group, start_total, jnp.arange(step_count, dtype=jnp.int32))
    return total.astype(jnp.bfloat16)


def solution(mesh):
    return jax.shard_map(
        body,
        mesh=mesh,
        in_specs=(
            P(("gx", "gy"), None, None),
            P(("gx", "gy"), None),
            P(("gx", "gy"), None, None),
            P(("gx", "gy"), None),
            P(("gx", "gy"), None, None),
            P(("gx", "gy")),
            P(("gx", "gy")),
        ),
        out_specs=P(("gx", "gy"), None, None),
        check_vma=False,
    )
```

profile of v0, /device:TPU:0, one launch (start us, length us, event | category | flops | bytes accessed | tf_op | source)
XLA Modules:
  0.0 651.3 jit_solution(14719270897375090564)
XLA Ops:
  6.7 10.3 %all-to-all-start = ((s32[32,1,1]{2,1,0:T(1,128)}), s32[32,1,1]{2,1,0:T(1,128)S(1)}, u32[]{:S(2)}, u32[]{:S(2)}) async-start(s32[32,1,1]{2,1,0:T(1,128)} %copy.17), calls=%async_computation | async-start | bytes 32768 | tf_op jit(solution)/shard_map/all_to_all | solution.py:42
  37.1 5.9 gather_fusion.3
  43.0 5.9 gather_fusion.4
  62.7 15.5 %gather_fusion.5 = bf16[64,512,384]{2,1,0:T(8,128)(2,1)} fusion(bf16[32,512,384]{2,1,0:T(8,128)(2,1)} %pad_maximum_fusion, s32[1024]{0:T(1024)S(1)} %pad_clamp_fusion.1), kind=kCustom, calls=%fused_computation.5 | custom fusion | bytes 50331904 | tf_op jit(solution)/shard_map/gather | solution.py:39
  78.2 9.3 %all-to-all-start.1 = ((bf16[32,2,512,384]{3,2,1,0:T(8,128)(2,1)}), bf16[32,2,512,384]{3,2,1,0:T(8,128)(2,1)}, u32[]{:S(2)}, u32[]{:S(2)}) async-start(bf16[32,2,512,384]{3,2,1,0:T(8,128)(2,1)} %bitcast.25), calls=%async_computation.1 | async-start | bytes 50331648 | tf_op jit(solution)/shard_map/all_to_all | solution.py:41
  88.3 320.6 %all-to-all-done.1 = bf16[32,2,512,384]{3,2,1,0:T(8,128)(2,1)} async-done(((bf16[32,2,512,384]{3,2,1,0:T(8,128)(2,1)}), bf16[32,2,512,384]{3,2,1,0:T(8,128)(2,1)}, u32[]{:S(2)}, u32[]{:S(2)}) %all-to-all-start.1) | async-done | bytes 25165856 | tf_op jit(solution)/shard_map/all_to_all | solution.py:41
  408.8 21.0 %broadcast_select_fusion = bf16[32,2,512,384]{3,2,1,0:T(8,128)(2,1)} fusion(bf16[32,2,512,384]{3,2,1,0:T(8,128)(2,1)} %all-to-all-done.1, pred[32,2]{1,0:T(8,128)(4,1)S(1)} %iota_compare_fusion.1), kind=kLoop, calls=%fused_computation.18 | loop fusion | flops 12582912 | bytes 50331712 | tf_op jit(solution)/shard_map/jit(_where)/select_n | solution.py:45
  429.8 220.2 %while.11 = (s32[]{:T(128)}, f32[8,512,128]{2,0,1:T(8,128)S(1)}, s32[8]{0:T(128)S(1)}, s32[128]{0:T(128)S(1)}, s32[128]{0:T(128)S(1)}, /*index=5*/bf16[64,512,38...) while((s32[]{:T(128)}, f32[8,512,128]{2,0,1:T(8,128)S(1)}, ...), condition=%wide.region_1.2_spmd.clone, body=%wide.region_0.1_spmd.clone.sunk | while | flops 907019456 | bytes 33034876 | solution.py:67
  431.1 12.3 %gather_fusion = bf16[16,512,384]{2,1,0:T(8,128)(2,1)} fusion(bf16[64,512,384]{2,1,0:T(8,128)(2,1)} %get-tuple-element.168, s32[1024]{0:T(1024)S(1)} %pad_clamp_fusion.7), kind=kCustom, calls=%fused_computation.clone.clone.1 | custom fusion | bytes 12582976 | tf_op jit(solution)/shard_map/while/body/eval_jaxpr/gather | solution.py:58
  443.4 7.0 %fusion.28 = f32[16,512,128]{2,1,0:T(8,128)} fusion(bf16[16,512,384]{2,1,0:T(8,128)(2,1)} %gather_fusion, bf16[128,384,128]{2,1,0:T(8,128)(2,1)} %get-tuple-element.169, s32[]{:T(128)S(6)} %select_n.66), kind=kOutput, calls=%fused_computation.10.clone.1 | convolution fusion | flops 805306368 | bytes 12058628 | tf_op jit(solution)/shard_map/while/body/eval_jaxpr/gcj,gjk->gck/dot_general | solution.py:59
  450.4 7.0 %select_add_fusion.2 = f32[8,512,128]{2,0,1:T(8,128)S(1)} fusion(f32[8,512,128]{2,0,1:T(8,128)S(1)} %get-tuple-element.153, f32[16,512,128]{2,1,0:T(8,128)} %fusion.28, pred[]{:T(512)S(6)} %compare.3, s32[16]{0:T(128)S(1)} %dynamic_slice.27), kind=kOutput, calls=%fused_computation.9.clone.1 | convolution fusion | flops 101712000 | bytes 8388673 | tf_op jit(solution)/shard_map/while/body/eval_jaxpr/og,gck->ock/dot_general | solution.py:61
  458.6 12.3 %gather_fusion = bf16[16,512,384]{2,1,0:T(8,128)(2,1)} fusion(bf16[64,512,384]{2,1,0:T(8,128)(2,1)} %get-tuple-element.168, s32[1024]{0:T(1024)S(1)} %pad_clamp_fusion.7), kind=kCustom, calls=%fused_computation.clone.clone.1 | custom fusion | bytes 12582976 | tf_op jit(solution)/shard_map/while/body/eval_jaxpr/gather | solution.py:58
  470.9 7.0 %fusion.28 = f32[16,512,128]{2,1,0:T(8,128)} fusion(bf16[16,512,384]{2,1,0:T(8,128)(2,1)} %gather_fusion, bf16[128,384,128]{2,1,0:T(8,128)(2,1)} %get-tuple-element.169, s32[]{:T(128)S(6)} %select_n.66), kind=kOutput, calls=%fused_computation.10.clone.1 | convolution fusion | flops 805306368 | bytes 12058628 | tf_op jit(solution)/shard_map/while/body/eval_jaxpr/gcj,gjk->gck/dot_general | solution.py:59
  477.9 7.0 %select_add_fusion.2 = f32[8,512,128]{2,0,1:T(8,128)S(1)} fusion(f32[8,512,128]{2,0,1:T(8,128)S(1)} %get-tuple-element.153, f32[16,512,128]{2,1,0:T(8,128)} %fusion.28, pred[]{:T(512)S(6)} %compare.3, s32[16]{0:T(128)S(1)} %dynamic_slice.27), kind=kOutput, calls=%fused_computation.9.clone.1 | convolution fusion | flops 101712000 | bytes 8388673 | tf_op jit(solution)/shard_map/while/body/eval_jaxpr/og,gck->ock/dot_general | solution.py:61
  486.1 12.3 %gather_fusion = bf16[16,512,384]{2,1,0:T(8,128)(2,1)} fusion(bf16[64,512,384]{2,1,0:T(8,128)(2,1)} %get-tuple-element.168, s32[1024]{0:T(1024)S(1)} %pad_clamp_fusion.7), kind=kCustom, calls=%fused_computation.clone.clone.1 | custom fusion | bytes 12582976 | tf_op jit(solution)/shard_map/while/body/eval_jaxpr/gather | solution.py:58
  498.4 7.0 %fusion.28 = f32[16,512,128]{2,1,0:T(8,128)} fusion(bf16[16,512,384]{2,1,0:T(8,128)(2,1)} %gather_fusion, bf16[128,384,128]{2,1,0:T(8,128)(2,1)} %get-tuple-element.169, s32[]{:T(128)S(6)} %select_n.66), kind=kOutput, calls=%fused_computation.10.clone.1 | convolution fusion | flops 805306368 | bytes 12058628 | tf_op jit(solution)/shard_map/while/body/eval_jaxpr/gcj,gjk->gck/dot_general | solution.py:59
  505.4 7.0 %select_add_fusion.2 = f32[8,512,128]{2,0,1:T(8,128)S(1)} fusion(f32[8,512,128]{2,0,1:T(8,128)S(1)} %get-tuple-element.153, f32[16,512,128]{2,1,0:T(8,128)} %fusion.28, pred[]{:T(512)S(6)} %compare.3, s32[16]{0:T(128)S(1)} %dynamic_slice.27), kind=kOutput, calls=%fused_computation.9.clone.1 | convolution fusion | flops 101712000 | bytes 8388673 | tf_op jit(solution)/shard_map/while/body/eval_jaxpr/og,gck->ock/dot_general | solution.py:61
  513.6 12.3 %gather_fusion = bf16[16,512,384]{2,1,0:T(8,128)(2,1)} fusion(bf16[64,512,384]{2,1,0:T(8,128)(2,1)} %get-tuple-element.168, s32[1024]{0:T(1024)S(1)} %pad_clamp_fusion.7), kind=kCustom, calls=%fused_computation.clone.clone.1 | custom fusion | bytes 12582976 | tf_op jit(solution)/shard_map/while/body/eval_jaxpr/gather | solution.py:58
  525.9 7.0 %fusion.28 = f32[16,512,128]{2,1,0:T(8,128)} fusion(bf16[16,512,384]{2,1,0:T(8,128)(2,1)} %gather_fusion, bf16[128,384,128]{2,1,0:T(8,128)(2,1)} %get-tuple-element.169, s32[]{:T(128)S(6)} %select_n.66), kind=kOutput, calls=%fused_computation.10.clone.1 | convolution fusion | flops 805306368 | bytes 12058628 | tf_op jit(solution)/shard_map/while/body/eval_jaxpr/gcj,gjk->gck/dot_general | solution.py:59
  533.0 7.0 %select_add_fusion.2 = f32[8,512,128]{2,0,1:T(8,128)S(1)} fusion(f32[8,512,128]{2,0,1:T(8,128)S(1)} %get-tuple-element.153, f32[16,512,128]{2,1,0:T(8,128)} %fusion.28, pred[]{:T(512)S(6)} %compare.3, s32[16]{0:T(128)S(1)} %dynamic_slice.27), kind=kOutput, calls=%fused_computation.9.clone.1 | convolution fusion | flops 101712000 | bytes 8388673 | tf_op jit(solution)/shard_map/while/body/eval_jaxpr/og,gck->ock/dot_general | solution.py:61
  541.2 12.3 %gather_fusion = bf16[16,512,384]{2,1,0:T(8,128)(2,1)} fusion(bf16[64,512,384]{2,1,0:T(8,128)(2,1)} %get-tuple-element.168, s32[1024]{0:T(1024)S(1)} %pad_clamp_fusion.7), kind=kCustom, calls=%fused_computation.clone.clone.1 | custom fusion | bytes 12582976 | tf_op jit(solution)/shard_map/while/body/eval_jaxpr/gather | solution.py:58
  553.5 7.0 %fusion.28 = f32[16,512,128]{2,1,0:T(8,128)} fusion(bf16[16,512,384]{2,1,0:T(8,128)(2,1)} %gather_fusion, bf16[128,384,128]{2,1,0:T(8,128)(2,1)} %get-tuple-element.169, s32[]{:T(128)S(6)} %select_n.66), kind=kOutput, calls=%fused_computation.10.clone.1 | convolution fusion | flops 805306368 | bytes 12058628 | tf_op jit(solution)/shard_map/while/body/eval_jaxpr/gcj,gjk->gck/dot_general | solution.py:59
  560.5 7.0 %select_add_fusion.2 = f32[8,512,128]{2,0,1:T(8,128)S(1)} fusion(f32[8,512,128]{2,0,1:T(8,128)S(1)} %get-tuple-element.153, f32[16,512,128]{2,1,0:T(8,128)} %fusion.28, pred[]{:T(512)S(6)} %compare.3, s32[16]{0:T(128)S(1)} %dynamic_slice.27), kind=kOutput, calls=%fused_computation.9.clone.1 | convolution fusion | flops 101712000 | bytes 8388673 | tf_op jit(solution)/shard_map/while/body/eval_jaxpr/og,gck->ock/dot_general | solution.py:61
  568.7 12.3 %gather_fusion = bf16[16,512,384]{2,1,0:T(8,128)(2,1)} fusion(bf16[64,512,384]{2,1,0:T(8,128)(2,1)} %get-tuple-element.168, s32[1024]{0:T(1024)S(1)} %pad_clamp_fusion.7), kind=kCustom, calls=%fused_computation.clone.clone.1 | custom fusion | bytes 12582976 | tf_op jit(solution)/shard_map/while/body/eval_jaxpr/gather | solution.py:58
  581.0 7.0 %fusion.28 = f32[16,512,128]{2,1,0:T(8,128)} fusion(bf16[16,512,384]{2,1,0:T(8,128)(2,1)} %gather_fusion, bf16[128,384,128]{2,1,0:T(8,128)(2,1)} %get-tuple-element.169, s32[]{:T(128)S(6)} %select_n.66), kind=kOutput, calls=%fused_computation.10.clone.1 | convolution fusion | flops 805306368 | bytes 12058628 | tf_op jit(solution)/shard_map/while/body/eval_jaxpr/gcj,gjk->gck/dot_general | solution.py:59
  588.0 7.0 %select_add_fusion.2 = f32[8,512,128]{2,0,1:T(8,128)S(1)} fusion(f32[8,512,128]{2,0,1:T(8,128)S(1)} %get-tuple-element.153, f32[16,512,128]{2,1,0:T(8,128)} %fusion.28, pred[]{:T(512)S(6)} %compare.3, s32[16]{0:T(128)S(1)} %dynamic_slice.27), kind=kOutput, calls=%fused_computation.9.clone.1 | convolution fusion | flops 101712000 | bytes 8388673 | tf_op jit(solution)/shard_map/while/body/eval_jaxpr/og,gck->ock/dot_general | solution.py:61
  596.2 12.3 %gather_fusion = bf16[16,512,384]{2,1,0:T(8,128)(2,1)} fusion(bf16[64,512,384]{2,1,0:T(8,128)(2,1)} %get-tuple-element.168, s32[1024]{0:T(1024)S(1)} %pad_clamp_fusion.7), kind=kCustom, calls=%fused_computation.clone.clone.1 | custom fusion | bytes 12582976 | tf_op jit(solution)/shard_map/while/body/eval_jaxpr/gather | solution.py:58
  608.5 7.0 %fusion.28 = f32[16,512,128]{2,1,0:T(8,128)} fusion(bf16[16,512,384]{2,1,0:T(8,128)(2,1)} %gather_fusion, bf16[128,384,128]{2,1,0:T(8,128)(2,1)} %get-tuple-element.169, s32[]{:T(128)S(6)} %select_n.66), kind=kOutput, calls=%fused_computation.10.clone.1 | convolution fusion | flops 805306368 | bytes 12058628 | tf_op jit(solution)/shard_map/while/body/eval_jaxpr/gcj,gjk->gck/dot_general | solution.py:59
  615.5 7.0 %select_add_fusion.2 = f32[8,512,128]{2,0,1:T(8,128)S(1)} fusion(f32[8,512,128]{2,0,1:T(8,128)S(1)} %get-tuple-element.153, f32[16,512,128]{2,1,0:T(8,128)} %fusion.28, pred[]{:T(512)S(6)} %compare.3, s32[16]{0:T(128)S(1)} %dynamic_slice.27), kind=kOutput, calls=%fused_computation.9.clone.1 | convolution fusion | flops 101712000 | bytes 8388673 | tf_op jit(solution)/shard_map/while/body/eval_jaxpr/og,gck->ock/dot_general | solution.py:61
  623.7 12.3 %gather_fusion = bf16[16,512,384]{2,1,0:T(8,128)(2,1)} fusion(bf16[64,512,384]{2,1,0:T(8,128)(2,1)} %get-tuple-element.168, s32[1024]{0:T(1024)S(1)} %pad_clamp_fusion.7), kind=kCustom, calls=%fused_computation.clone.clone.1 | custom fusion | bytes 12582976 | tf_op jit(solution)/shard_map/while/body/eval_jaxpr/gather | solution.py:58
  636.0 7.0 %fusion.28 = f32[16,512,128]{2,1,0:T(8,128)} fusion(bf16[16,512,384]{2,1,0:T(8,128)(2,1)} %gather_fusion, bf16[128,384,128]{2,1,0:T(8,128)(2,1)} %get-tuple-element.169, s32[]{:T(128)S(6)} %select_n.66), kind=kOutput, calls=%fused_computation.10.clone.1 | convolution fusion | flops 805306368 | bytes 12058628 | tf_op jit(solution)/shard_map/while/body/eval_jaxpr/gcj,gjk->gck/dot_general | solution.py:59
  643.1 7.0 %select_add_fusion.2 = f32[8,512,128]{2,0,1:T(8,128)S(1)} fusion(f32[8,512,128]{2,0,1:T(8,128)S(1)} %get-tuple-element.153, f32[16,512,128]{2,1,0:T(8,128)} %fusion.28, pred[]{:T(512)S(6)} %compare.3, s32[16]{0:T(128)S(1)} %dynamic_slice.27), kind=kOutput, calls=%fused_computation.9.clone.1 | convolution fusion | flops 101712000 | bytes 8388673 | tf_op jit(solution)/shard_map/while/body/eval_jaxpr/og,gck->ock/dot_general | solution.py:61
  (71 shorter events, 48.2 us)
Async XLA Ops:
  2.7 15.9 %collective-permute-start = (bf16[8,512,128]{2,1,0:T(8,128)(2,1)}, bf16[8,512,128]{2,1,0:T(8,128)(2,1)S(1)}, u32[]{:S(2)}, u32[]{:S(2)}) collective-permute-start(bf16[8,512,128]{2,1,0:T(8,128)(2,1)} %get-tuple-element.89), channel_id=1, source_target_pairs={{0,1},{1,2},{2,3},{3,4},{4,5},{5,6},{6,7},{7,8},{8,9},{9,10},{10,1... | collective-permute-start | bytes 3145736 | tf_op jit(solution)/shard_map/ppermute | solution.py:12
  4.0 20.3 %collective-permute-start.1 = (bf16[8,512,128]{2,1,0:T(8,128)(2,1)S(1)}, bf16[8,512,128]{2,1,0:T(8,128)(2,1)S(1)}, u32[]{:S(2)}, u32[]{:S(2)}) collective-permute-start(bf16[8,512,128]{2,1,0:T(8,128)(2,1)S(1)} %get-tuple-element.88), channel_id=1, source_target_pairs={{1,0},{2,1},{3,2},{4,3},{5,4},{6,5},{7,6},{8,7},{9,8},{10,9},{11,1... | collective-permute-start | bytes 3145736 | tf_op jit(solution)/shard_map/ppermute | solution.py:15
  6.7 71.5 %all-to-all-start = ((s32[32,1,1]{2,1,0:T(1,128)}), s32[32,1,1]{2,1,0:T(1,128)S(1)}, u32[]{:S(2)}, u32[]{:S(2)}) async-start(s32[32,1,1]{2,1,0:T(1,128)} %copy.17), calls=%async_computation | async-start | bytes 32768 | tf_op jit(solution)/shard_map/all_to_all | solution.py:42
  48.9 5.1 copy-start.1
  48.9 5.9 copy-start.2
  54.8 2.2 copy-start
  78.2 330.7 %all-to-all-start.1 = ((bf16[32,2,512,384]{3,2,1,0:T(8,128)(2,1)}), bf16[32,2,512,384]{3,2,1,0:T(8,128)(2,1)}, u32[]{:S(2)}, u32[]{:S(2)}) async-start(bf16[32,2,512,384]{3,2,1,0:T(8,128)(2,1)} %bitcast.25), calls=%async_computation.1 | async-start | bytes 50331648 | tf_op jit(solution)/shard_map/all_to_all | solution.py:41
  88.2 341.6 %copy-start.3 = (s32[128]{0:T(128)S(1)}, s32[128]{0:T(128)}, u32[]{:S(2)}) copy-start(s32[128]{0:T(128)} %param.14) | copy-start | bytes 1540
  88.2 341.6 %copy-start.4 = (s32[128]{0:T(128)S(1)}, s32[128]{0:T(128)}, u32[]{:S(2)}) copy-start(s32[128]{0:T(128)} %param.15) | copy-start | bytes 1540
where the time goes:
time: 654 us; the launch traced here: 651 us
  waiting for transfers between devices  321 us (49%)
  local copies, waits for them, and re-layouts  156 us (24%)
  matrix products  111 us (17%)
  other arithmetic  35.8 us (5%)
  starting transfers between devices  22.3 us (3%)
    all_to_all x1, waiting for transfers between devices, body(): lax.all_to_all(outgoing, 'gy', split_axis=0, concat_axis=0, tiled=True)  321 us
    gather x8, local copies, waits for them, and re-layouts, add_group(): chosen = received[column_index]  98.2 us
    dot_general x8, matrix products, add_group(): jnp.einsum('gcj,gjk->gck', chosen, weights, preferred_element_type=jnp.fl...  55.8 us
    dot_general x8, matrix products, add_group(): jnp.einsum('og,gck->ock', selector, products, precision=lax.Precision.HIG...  55.6 us
    select_n x1, other arithmetic, body(): jnp.where(occupied[:, :, None, None], incoming, jnp.zeros_like(incoming))  21 us
    gather x1, local copies, waits for them, and re-layouts, body(): payload[slot_order]  15.5 us
  transfers between devices with their start and end apart: 4, of which 1 were waited for; matrix products, arithmetic and copies ran while one was open for 10% of the time, Pallas kernels for 0%

commit v1 on v0

v1 whole, which is shorter than its diff:
```python
import functools

import jax
import jax.numpy as jnp
from jax import lax
from jax.experimental import pallas as pl
from jax.experimental.pallas import tpu as pltpu
from jax.sharding import PartitionSpec as P

VMEM_LIMIT = 48 * 1024 * 1024
DEPTH = 8
NOTE = 16


def any_spec():
    return pl.BlockSpec(memory_space=pl.ANY)


def smem_spec():
    return pl.BlockSpec(memory_space=pltpu.SMEM)


def neighbour_blocks(block, width):
    axes = ("gx", "gy")
    count = lax.axis_size(axes)
    forward = [(i, i + 1) for i in range(count - 1)]
    backward = [(target, source) for source, target in forward]
    low = lax.ppermute(block[-width:], axes, forward)
    high = lax.ppermute(block[:width], axes, backward)
    return low, high


def order_kernel(slots, note, source, target, held, sems):
    count = target.shape[0]
    columns = source.shape[1]
    held[:, columns:, :] = jnp.broadcast_to(note[...][:, None, :], (count, NOTE, note.shape[1]))

    def fetch(i):
        return pltpu.make_async_copy(
            source.at[slots[i]], held.at[i, pl.ds(0, columns)], sems.at[0, i]
        )

    def store(i):
        return pltpu.make_async_copy(held.at[i], target.at[i], sems.at[1, i])

    def begin(i, carry):
        fetch(i).start()
        return carry

    def turn(i, carry):
        fetch(i).wait()
        store(i).start()
        return carry

    def end(i, carry):
        store(i).wait()
        return carry

    lax.fori_loop(0, count, begin, 0)
    lax.fori_loop(0, count, turn, 0)
    lax.fori_loop(0, count, end, 0)


def in_order(blocks, slots, note):
    count = slots.shape[0]
    shape = (count, blocks.shape[1] + NOTE, blocks.shape[2])
    return pl.pallas_call(
        order_kernel,
        out_shape=jax.ShapeDtypeStruct(shape, blocks.dtype),
        in_specs=[smem_spec(), pl.BlockSpec(memory_space=pltpu.VMEM), any_spec()],
        out_specs=any_spec(),
        scratch_shapes=[
            pltpu.VMEM(shape, blocks.dtype),
            pltpu.SemaphoreType.DMA((2, count)),
        ],
        compiler_params=pltpu.CompilerParams(vmem_limit_bytes=VMEM_LIMIT),
        cost_estimate=pl.CostEstimate(
            flops=0, transcendentals=0, bytes_accessed=4 * count * shape[1] * shape[2]
        ),
        name="order",
    )(slots, note, blocks)


def gradient_kernel(slots, near, low, own, high, target, held, made, sems, out_sems):
    count, columns, cells = own.shape
    width = low.shape[0]
    steps = target.shape[0]
    copies = [
        pltpu.make_async_copy(low, held.at[pl.ds(0, width)], sems.at[0]),
        pltpu.make_async_copy(own, held.at[pl.ds(width, count)], sems.at[1]),
        pltpu.make_async_copy(high, held.at[pl.ds(width + count, width)], sems.at[2]),
    ]
    for copy in copies:
        copy.start()
    for copy in copies:
        copy.wait()

    def make(i):
        block = slots[i]
        for axis in range(2):
            first = near[4 * block + 2 * axis]
            second = near[4 * block + 2 * axis + 1]
            for begin in range(0, columns, 128):
                rows = pl.ds(begin, 128)
                a = held[first, rows, :].astype(jnp.float32)
                b = held[second, rows, :].astype(jnp.float32)
                made[i, rows, axis * cells : (axis + 1) * cells] = (0.5 * (a - b)).astype(made.dtype)

    def store(i):
        return pltpu.make_async_copy(made.at[i], target.at[i], out_sems.at[i])

    def turn(i, carry):
        make(i)
        store(i).start()
        return carry

    def end(i, carry):
        store(i).wait()
        return carry

    lax.fori_loop(0, steps, turn, 0)
    lax.fori_loop(0, steps, end, 0)


def gradients(slots, near, low, own, high):
    width = low.shape[0]
    count, columns, cells = own.shape
    steps = slots.shape[0]
    return pl.pallas_call(
        gradient_kernel,
        out_shape=jax.ShapeDtypeStruct((steps, columns, 2 * cells), own.dtype),
        in_specs=[smem_spec(), smem_spec()] + [any_spec()] * 3,
        out_specs=any_spec(),
        scratch_shapes=[
            pltpu.VMEM((count + 2 * width, columns, cells), own.dtype),
            pltpu.VMEM((steps, columns, 2 * cells), own.dtype),
            pltpu.SemaphoreType.DMA((3,)),
            pltpu.SemaphoreType.DMA((steps,)),
        ],
        compiler_params=pltpu.CompilerParams(vmem_limit_bytes=VMEM_LIMIT),
        cost_estimate=pl.CostEstimate(
            flops=4 * steps * columns * cells, transcendentals=0, bytes_accessed=16 * 1024 * 1024
        ),
        name="gradients",
    )(slots, near, low, own, high)


def payload_kernel(where, low, own, high, target, held, sems):
    count, columns, cells = own.shape
    width = low.shape[0]

    def each(act):
        for i in range(5):
            index = where[i]

            @pl.when(index < width)
            def from_low():
                act(pltpu.make_async_copy(low.at[index], held.at[i], sems.at[i]))

            @pl.when((index >= width) & (index < width + count))
            def from_own():
                act(pltpu.make_async_copy(own.at[index - width], held.at[i], sems.at[i]))

            @pl.when(index >= width + count)
            def from_high():
                act(pltpu.make_async_copy(high.at[index - width - count], held.at[i], sems.at[i]))

    each(lambda copy: copy.start())
    each(lambda copy: copy.wait())
    target[0, :, :cells] = held[0]
    for axis in range(2):
        for begin in range(0, columns, 128):
            rows = pl.ds(begin, 128)
            a = held[1 + 2 * axis, rows, :].astype(jnp.float32)
            b = held[2 + 2 * axis, rows, :].astype(jnp.float32)
            target[0, rows, (axis + 1) * cells : (axis + 2) * cells] = (0.5 * (a - b)).astype(
                target.dtype
            )


def one_payload(where, low, own, high):
    count, columns, cells = own.shape
    return pl.pallas_call(
        payload_kernel,
        out_shape=jax.ShapeDtypeStruct((1, columns, 3 * cells), own.dtype),
        in_specs=[smem_spec()] + [any_spec()] * 3,
        out_specs=pl.BlockSpec(memory_space=pltpu.VMEM),
        scratch_shapes=[
            pltpu.VMEM((5, columns, cells), own.dtype),
            pltpu.SemaphoreType.DMA((5,)),
        ],
        cost_estimate=pl.CostEstimate(flops=0, transcendentals=0, bytes_accessed=1024 * 1024),
        name="payload",
    )(where, low, own, high)


def remap_kernel(first_row, depth_k, has_total, final, plan, *refs):
    if has_total:
        total_in, received, weights, out, total, fields, tiles, order, sems, total_sem = refs
    else:
        received, weights, out, total, fields, tiles, order, sems, total_sem = refs
    sources = received.shape[0]
    columns = total.shape[1]
    cells = weights.shape[2]

    def note(q, live):
        order[live] = q
        return live + plan[q]

    live = lax.fori_loop(0, sources, note, 0)

    def copies(j):
        q = order[j]
        place = lax.rem(j, DEPTH)
        first = lax.shift_right_logical(plan[sources + q], 3)
        second = lax.shift_right_logical(plan[2 * sources + q], 3)
        rows = pl.ds(first_row, depth_k)
        return (
            pltpu.make_async_copy(
                received.at[q, pl.ds(0, columns)], fields.at[place], sems.at[0, place]
            ),
            pltpu.make_async_copy(
                weights.at[first, rows], tiles.at[place, :, pl.ds(0, cells)], sems.at[1, place]
            ),
            pltpu.make_async_copy(
                weights.at[second, rows], tiles.at[place, :, pl.ds(cells, cells)], sems.at[2, place]
            ),
        )

    def start(j, carry):
        for copy in copies(j):
            copy.start()
        return carry

    lax.fori_loop(0, jnp.minimum(live, DEPTH), start, 0)
    if has_total:
        copy = pltpu.make_async_copy(total_in, total, total_sem.at[0])
        copy.start()
        copy.wait()
    else:
        total[...] = jnp.zeros_like(total)

    part = min(columns, 256)

    def add(j, carry):
        for copy in copies(j):
            copy.wait()
        q = order[j]
        place = lax.rem(j, DEPTH)
        first_ocean = plan[sources + q] & 7
        second_ocean = plan[2 * sources + q] & 7
        for begin in range(0, columns, part):
            rows = pl.ds(begin, part)
            product = jnp.dot(
                fields[place, rows, :], tiles[place], preferred_element_type=jnp.float32
            )
            total[first_ocean, rows, :] += product[:, :cells]
            total[second_ocean, rows, :] += product[:, cells:]

        @pl.when(j + DEPTH < live)
        def more():
            start(j + DEPTH, 0)

        return carry

    lax.fori_loop(0, live, add, 0)
    out[...] = total[...].astype(out.dtype)


def remap(plan, received, weights, total, first_row, ocean_count, columns, final):
    sources, unused, depth_k = received.shape
    cells = weights.shape[2]
    shape = (ocean_count, columns, cells)
    whole = pl.BlockSpec(memory_space=pltpu.VMEM)
    has_total = total is not None
    kernel = functools.partial(remap_kernel, first_row, depth_k, has_total, final)
    return pl.pallas_call(
        kernel,
        out_shape=jax.ShapeDtypeStruct(shape, jnp.bfloat16 if final else jnp.float32),
        in_specs=[smem_spec()] + [any_spec()] * has_total + [any_spec(), any_spec()],
        out_specs=whole,
        scratch_shapes=[
            pltpu.VMEM(shape, jnp.float32),
            pltpu.VMEM((DEPTH, columns, depth_k), received.dtype),
            pltpu.VMEM((DEPTH, depth_k, 2 * cells), weights.dtype),
            pltpu.SMEM((sources + 1,), jnp.int32),
            pltpu.SemaphoreType.DMA((3, DEPTH)),
            pltpu.SemaphoreType.DMA((1,)),
        ],
        compiler_params=pltpu.CompilerParams(vmem_limit_bytes=VMEM_LIMIT),
        cost_estimate=pl.CostEstimate(
            flops=4 * sources * columns * depth_k * cells,
            transcendentals=0,
            bytes_accessed=2 * sources * columns * depth_k * 2,
        ),
        name="remap",
    )(plan, *([total] if has_total else []), received, weights)


def body(atm_fields, neighbours, send_slots, send_counts, tile_weights, tile_rows, tile_cols):
    block_count, column_count, cell_count = atm_fields.shape
    peers = lax.axis_size("gy")
    ocean_count = block_count // 4
    tile_count = tile_weights.shape[0]
    halo_width = block_count // 4
    slots = send_slots.reshape(peers, -1)
    own_counts = send_counts.reshape(peers)
    me = lax.axis_index("gy")

    def exchange(blocks):
        return lax.all_to_all(blocks, "gy", split_axis=0, concat_axis=0, tiled=True)

    doubled = own_counts >= 2
    before = jnp.cumsum(doubled.astype(jnp.int32))
    overflow = jnp.sum(jnp.where(doubled & (before == 1), slots[:, 1], 0))
    low, high = neighbour_blocks(atm_fields, halo_width)
    facts = jnp.stack([own_counts, before, jnp.broadcast_to(before[-1], before.shape)], axis=1)
    note = jnp.pad(facts.astype(atm_fields.dtype), ((0, 0), (0, cell_count - 3)))
    near = neighbours - (lax.axis_index(("gx", "gy")) * block_count - halo_width)
    where = jnp.concatenate([overflow[None] + halo_width, near[overflow]])
    near = near.reshape(-1)
    values = exchange(in_order(atm_fields, slots[:, 0], note))
    spares = lax.all_gather(
        one_payload(where, low, atm_fields, high), "gy", axis=0, tiled=True
    )
    slopes = gradients(slots[:, 0], near, low, atm_fields, high)
    slopes, values = lax.optimization_barrier((slopes, values))
    slopes = exchange(slopes)

    told = values[:, column_count, :3].astype(jnp.int32)
    arrived, rank = told[:, 0], told[:, 1]
    most = jnp.max(told[:, 2])
    planes = lax.axis_size("gx")
    ahead = [
        lax.ppermute(most, "gx", [(i, (i + step) % planes) for i in range(planes)])
        for step in range(1, planes)
    ]
    for other in ahead:
        most = jnp.maximum(most, other)
    slot_ids = lax.broadcasted_iota(jnp.int32, (2 * peers, tile_count), 0)
    codes = lax.broadcasted_iota(jnp.int32, (2 * peers, tile_count), 1) * 8 + tile_rows[None, :]
    named = slot_ids == tile_cols[None, :]
    first_code = jnp.min(jnp.where(named, codes, 8 * tile_count), axis=1).reshape(peers, 2)
    second_code = jnp.max(jnp.where(named, codes, -1), axis=1).reshape(peers, 2)

    def plan(live, slot):
        return jnp.concatenate([live.astype(jnp.int32), first_code[:, slot], second_code[:, slot]])

    plan_first = plan(arrived >= 1, 0)
    plan_spare = plan((arrived >= 2) & (rank == 1), 1)
    plan_rest = plan((arrived >= 2) & (rank > 1), 1)

    def add(this_plan, received, total, first_row, final=False):
        return remap(
            this_plan, received, tile_weights, total, first_row, ocean_count, column_count, final
        )

    total = add(plan_first, values, None, 0)
    total = add(plan_spare, spares, total, 0)

    def finish(total):
        return add(plan_first, slopes, total, cell_count, final=True)

    def with_rest(total, unused):
        rest_slopes = gradients(slots[:, 1], near, low, atm_fields, high)
        total = add(plan_rest, exchange(in_order(atm_fields, slots[:, 1], note)), total, 0)
        return finish(add(plan_rest, exchange(rest_slopes), total, cell_count))

    return lax.cond(most > 1, with_rest, lambda unused, done: done, total, finish(total))


def solution(mesh):
    return jax.shard_map(
        body,
        mesh=mesh,
        in_specs=(
            P(("gx", "gy"), None, None),
            P(("gx", "gy"), None),
            P(("gx", "gy"), None, None),
            P(("gx", "gy"), None),
            P(("gx", "gy"), None, None),
            P(("gx", "gy")),
            P(("gx", "gy")),
        ),
        out_specs=P(("gx", "gy"), None, None),
        check_vma=False,
    )
```

time: 654 us -> 256 us (0.39)
  waiting for transfers between devices: 321 us -> 147 us
  local copies, waits for them, and re-layouts: 156 us -> 7.54 us
  matrix products: 111 us -> 0 us
  Pallas kernels: 0 us -> 41.8 us
  other arithmetic: 35.8 us -> 5.59 us
  between operations: 0.14 us -> 19.2 us
  starting transfers between devices: 22.3 us -> 36.4 us
    all_to_all x2, waiting for transfers between devices: 321 us -> 99.6 us  [exchange(): return lax.all_to_all(blocks, 'gy', split_axis=0, concat_axis=0, tiled=True)]
    gather x13 -> x0, local copies, waits for them, and re-layouts: 137 us -> none  [the longest x8 98.2 us: add_group(): chosen = received[column_index]]
    dot_general x16 -> x0, matrix products: 111 us -> none  [the longest x8 55.8 us: add_group(): jnp.einsum('gcj,gjk->gck', chosen, weights, preferred_element_type=jnp.fl...]
    all_gather x0 -> x1, waiting for transfers between devices: none -> 47.2 us  [body(): lax.all_gather(one_payload(where, low, atm_fields, high), 'gy', axis=0, t...]
    pallas_call x0 -> x6, Pallas kernels: none -> 41.8 us  [the longest x3 24.1 us: remap(): pl.pallas_call(kernel, out_shape=jax.ShapeDtypeStruct(shape, jnp.bfloat16...]
    select_n x11 -> x0, other arithmetic: 21.7 us -> none  [the longest x1 21 us: body(): jnp.where(occupied[:, :, None, None], incoming, jnp.zeros_like(incoming))]
    all_to_all x2, starting transfers between devices: 19.7 us -> 27.7 us  [exchange(): return lax.all_to_all(blocks, 'gy', split_axis=0, concat_axis=0, tiled=True)]
  transfers between devices with their start and end apart: 4 -> 8, of which waited for: 1 -> 3; matrix products, arithmetic and copies ran while one was open for 10% -> 3% of each run, Pallas kernels for 0% -> 10%
where the time goes in v1:
time: 256 us; the launch traced here: 257 us
  waiting for transfers between devices  147 us (57%)
  Pallas kernels  41.8 us (16%)
  starting transfers between devices  36.4 us (14%)
  between operations  19.2 us (8%)
  local copies, waits for them, and re-layouts  7.54 us (3%)
  other arithmetic  5.59 us (2%)
    all_to_all x2, waiting for transfers between devices, exchange(): return lax.all_to_all(blocks, 'gy', split_axis=0, concat_axis=0, tiled=True)  99.6 us
    all_gather x1, waiting for transfers between devices, body(): lax.all_gather(one_payload(where, low, atm_fields, high), 'gy', axis=0, t...  47.2 us
    all_to_all x2, starting transfers between devices, exchange(): return lax.all_to_all(blocks, 'gy', split_axis=0, concat_axis=0, tiled=True)  27.7 us
    pallas_call x3, Pallas kernels, remap(): pl.pallas_call(kernel, out_shape=jax.ShapeDtypeStruct(shape, jnp.bfloat16...  24.1 us
    pallas_call x1, Pallas kernels, in_order(): pl.pallas_call(order_kernel, out_shape=jax.ShapeDtypeStruct(shape, blocks...  8.02 us
    pallas_call x1, Pallas kernels, gradients(): pl.pallas_call(gradient_kernel, out_shape=jax.ShapeDtypeStruct((steps, co...  6.94 us
    ppermute x3, starting transfers between devices, body(): lax.ppermute(most, 'gx', [(i, (i + step) % planes) for i in range(planes)])  5.95 us
  transfers between devices with their start and end apart: 8, of which 3 were waited for; matrix products, arithmetic and copies ran while one was open for 3% of the time, Pallas kernels for 10%

profile of v1, /device:TPU:0, one launch (start us, length us, event | category | flops | bytes accessed | tf_op | source)
XLA Modules:
  0.0 257.4 jit_solution(14192811739268451862)
XLA Ops:
  6.5 2.6 %fusion.3 = (bf16[8,512,128]{2,1,0:T(8,128)(2,1)S(1)}, bf16[8,512,128]{2,1,0:T(8,128)(2,1)}) fusion(bf16[32,512,128]{2,1,0:T(8,128)(2,1)} %own.3), kind=kLoop, calls=%fused_computation.30 | loop fusion | bytes 4194304 | tf_op jit(solution)/shard_map/slice | solution.py:29
  9.2 1.5 collective-permute-start
  10.7 1.3 collective-permute-start.1
  12.0 0.7 fusion.1
  12.8 0.1 compare_reduce_fusion
  12.9 1.3 fusion.2
  16.5 0.7 broadcast_subtract_fusion
  17.2 0.2 dynamic-slice_reduce_fusion
  17.3 0.6 pad_add_fusion.1.where
  17.9 2.8 %payload.1 = bf16[1,512,384]{2,1,0:T(8,128)(2,1)} custom-call(s32[5]{0:T(128)} %pad_add_fusion.1.where, bf16[8,512,128]{2,1,0:T(8,128)(2,1)S(1)} %collective-permute-done.low, bf16[32,512,128]{2,1,0:T(8,128)(2,1)} %own.3, bf16[8,512,128]{2,1,0:T(8,128)(2,1)S(1)} %collective-permute-done.1.high), custom_call_target="tpu_custom_call" | custom-call | bytes 1048576 | tf_op jit(solution)/shard_map/payload/pallas_call | solution.py:183
  20.8 0.6 slice.60
  22.4 8.0 %order.3 = bf16[32,528,128]{2,1,0:T(8,128)(2,1)S(1)} custom-call(s32[32]{0:T(128)S(1)} %slice_bitcast_fusion.1.slots, bf16[32,128]{1,0:T(8,128)(2,1)S(1)} %pad.4.note, bf16[32,512,128]{2,1,0:T(8,128)(2,1)} %own.3), custom_call_target="tpu_custom_call" | custom-call | bytes 8650752 | tf_op jit(solution)/shard_map/order/pallas_call | solution.py:67
  30.4 2.0 copy-done
  32.4 21.9 %all-to-all-start.2 = ((bf16[32,528,128]{2,1,0:T(8,128)(2,1)}), bf16[32,528,128]{2,1,0:T(8,128)(2,1)}, u32[]{:S(2)}, u32[]{:S(2)}) async-start(bf16[32,528,128]{2,1,0:T(8,128)(2,1)} %copy-done), calls=%async_computation.2 | async-start | bytes 8650752 | tf_op jit(solution)/shard_map/all_to_all | solution.py:311
  54.5 6.9 %gradients.3 = bf16[32,512,256]{2,1,0:T(8,128)(2,1)} custom-call(s32[32]{0:T(128)S(1)} %slice_bitcast_fusion.1.slots, s32[128]{0:T(128)S(1)} %reshape.58.near, bf16[8,512,128]{2,1,0:T(8,128)(2,1)S(1)} %collective-permute-done.low, bf16[32,512,128]{2,1,0:T(8,128)(2,1)} %own.3, bf16[8,512,128]{2,1,0:T(8,128)(2,1)S(1)} %collective-permute-done.1.high), custom_call_target="tpu_custom_call" | custom-call | flops 8388608 | bytes 16777216 | tf_op jit(solution)/shard_map/gradients/pallas_call | solution.py:129
  61.4 53.7 %all-to-all-done.2.refs_0_ = bf16[32,528,128]{2,1,0:T(8,128)(2,1)} async-done(((bf16[32,528,128]{2,1,0:T(8,128)(2,1)}), bf16[32,528,128]{2,1,0:T(8,128)(2,1)}, u32[]{:S(2)}, u32[]{:S(2)}) %all-to-all-start.2) | async-done | bytes 4325408 | tf_op jit(solution)/shard_map/all_to_all | solution.py:311
  115.2 5.9 %all-to-all-start.3 = ((bf16[32,512,256]{2,1,0:T(8,128)(2,1)}), bf16[32,512,256]{2,1,0:T(8,128)(2,1)}, u32[]{:S(2)}, u32[]{:S(2)}) async-start(bf16[32,512,256]{2,1,0:T(8,128)(2,1)} %gradients.3), calls=%async_computation.3 | async-start | bytes 16777216 | tf_op jit(solution)/shard_map/all_to_all | solution.py:311
  121.1 0.1 select_reduce_fusion.1
  121.4 0.2 slice_reduce_fusion
  121.6 0.9 slice_convert_fusion
  122.6 0.7 fusion.4
  123.3 1.7 collective-permute-start.2
  125.0 1.6 collective-permute-start.3
  126.6 2.6 %collective-permute-start.4 = (s32[]{:T(128)}, s32[]{:T(128)}, u32[]{:S(2)}, u32[]{:S(2)}) collective-permute-start(s32[]{:T(128)} %get-tuple-element.59), channel_id=1, source_target_pairs={{0,96},{32,0},{64,32},{96,64},{1,97},{33,1},{65,33},{97,65},{2,98}... | collective-permute-start | bytes 20 | tf_op jit(solution)/shard_map/ppermute | solution.py:335
  129.4 0.1 convert_reduce_fusion.2
  129.6 9.4 %remap.9.refs_0_ = f32[8,512,128]{2,1,0:T(8,128)S(1)} custom-call(s32[96]{0:T(128)S(1)} %pad_add_fusion.plan, bf16[32,528,128]{2,1,0:T(8,128)(2,1)} %all-to-all-done.2.refs_0_, bf16[128,384,128]{2,1,0:T(8,128)(2,1)} %refs_2_.3), custom_call_target="tpu_custom_call" | custom-call | flops 1073741824 | bytes 8388608 | tf_op jit(solution)/shard_map/remap/pallas_call | solution.py:277
  139.1 0.1 convert_reduce_fusion
  141.9 47.2 %all-gather.2.cloned.1.call-done.refs_1_ = bf16[32,512,384]{2,1,0:T(8,128)(2,1)} async-done(((bf16[1,512,384]{2,1,0:T(8,128)(2,1)}), bf16[32,512,384]{2,1,0:T(8,128)(2,1)}) %all-gather.2.cloned.1.call-update) | async-done | bytes 12582928 | tf_op jit(solution)/shard_map/all_gather | solution.py:323
  189.0 2.6 remap.10.refs_0_
  191.6 45.9 %all-to-all-done.3.refs_1_ = bf16[32,512,256]{2,1,0:T(8,128)(2,1)} async-done(((bf16[32,512,256]{2,1,0:T(8,128)(2,1)}), bf16[32,512,256]{2,1,0:T(8,128)(2,1)}, u32[]{:S(2)}, u32[]{:S(2)}) %all-to-all-start.3) | async-done | bytes 8388640 | tf_op jit(solution)/shard_map/all_to_all | solution.py:311
  237.5 12.1 %remap.11 = bf16[8,512,128]{2,1,0:T(8,128)(2,1)S(1)} custom-call(s32[96]{0:T(128)S(1)} %pad_add_fusion.plan, f32[8,512,128]{2,1,0:T(8,128)} %remap.10.refs_0_, bf16[32,512,256]{2,1,0:T(8,128)(2,1)} %all-to-all-done.3.refs_1_, bf16[128,384,128]{2,1,0:T(8,128)(2,1)} %refs_2_.3), custom_call_target="tpu_custom_call" | custom-call | flops 2147483648 | bytes 16777216 | tf_op jit(solution)/shard_map/remap/pallas_call | solution.py:277
  249.6 1.0 copy-done.6
  (43 shorter events, 1.3 us)
Async XLA Ops:
  6.5 182.5 %all-gather.2.cloned.1.call-start = ((), (), s32[]{:S(2)}) async-start(), calls=%async_computation.4 | async-start | bytes 12976128 | tf_op jit(solution)/shard_map/all_gather | solution.py:323
  9.2 12.9 %copy-start.7 = (s32[1,32]{1,0:T(1,128)S(1)}, s32[1,32]{1,0:T(1,128)}, u32[]{:S(2)}) copy-start(s32[1,32]{1,0:T(1,128)} %param.12) | copy-start | bytes 388
  9.2 13.2 %copy-start.9 = (s32[1,32,2]{1,2,0:T(2,128)S(1)}, s32[1,32,2]{1,2,0:T(2,128)}, u32[]{:S(2)}) copy-start(s32[1,32,2]{1,2,0:T(2,128)} %param.11) | copy-start | bytes 772
  9.2 8.7 %collective-permute-start = (bf16[8,512,128]{2,1,0:T(8,128)(2,1)}, bf16[8,512,128]{2,1,0:T(8,128)(2,1)S(1)}, u32[]{:S(2)}, u32[]{:S(2)}) collective-permute-start(bf16[8,512,128]{2,1,0:T(8,128)(2,1)} %get-tuple-element.56), channel_id=1, source_target_pairs={{0,1},{1,2},{2,3},{3,4},{4,5},{5,6},{6,7},{7,8},{8,9},{9,10},{10,1... | collective-permute-start | bytes 3145736 | tf_op jit(solution)/shard_map/ppermute | solution.py:28
  10.7 7.3 %collective-permute-start.1 = (bf16[8,512,128]{2,1,0:T(8,128)(2,1)S(1)}, bf16[8,512,128]{2,1,0:T(8,128)(2,1)S(1)}, u32[]{:S(2)}, u32[]{:S(2)}) collective-permute-start(bf16[8,512,128]{2,1,0:T(8,128)(2,1)S(1)} %get-tuple-element.55), channel_id=1, source_target_pairs={{1,0},{2,1},{3,2},{4,3},{5,4},{6,5},{7,6},{8,7},{9,8},{10,9},{11,1... | collective-permute-start | bytes 3145736 | tf_op jit(solution)/shard_map/ppermute | solution.py:29
  17.9 36.5 %copy-start.4 = (bf16[8,512,128]{2,1,0:T(8,128)(2,1)}, bf16[8,512,128]{2,1,0:T(8,128)(2,1)S(1)}, u32[]{:S(2)}) copy-start(bf16[8,512,128]{2,1,0:T(8,128)(2,1)S(1)} %collective-permute-done.1.high) | copy-start | bytes 3145732
  30.4 2.0 copy-start
  32.4 82.8 %all-to-all-start.2 = ((bf16[32,528,128]{2,1,0:T(8,128)(2,1)}), bf16[32,528,128]{2,1,0:T(8,128)(2,1)}, u32[]{:S(2)}, u32[]{:S(2)}) async-start(bf16[32,528,128]{2,1,0:T(8,128)(2,1)} %copy-done), calls=%async_computation.2 | async-start | bytes 8650752 | tf_op jit(solution)/shard_map/all_to_all | solution.py:311
  61.4 59.6 %copy-start.10 = (s32[128]{0:T(128)S(1)}, s32[128]{0:T(128)}, u32[]{:S(2)}) copy-start(s32[128]{0:T(128)} %param.14) | copy-start | bytes 1540
  61.4 59.6 %copy-start.8 = (s32[128]{0:T(128)S(1)}, s32[128]{0:T(128)}, u32[]{:S(2)}) copy-start(s32[128]{0:T(128)} %param.15) | copy-start | bytes 1540
  115.2 122.3 %all-to-all-start.3 = ((bf16[32,512,256]{2,1,0:T(8,128)(2,1)}), bf16[32,512,256]{2,1,0:T(8,128)(2,1)}, u32[]{:S(2)}, u32[]{:S(2)}) async-start(bf16[32,512,256]{2,1,0:T(8,128)(2,1)} %gradients.3), calls=%async_computation.3 | async-start | bytes 16777216 | tf_op jit(solution)/shard_map/all_to_all | solution.py:311
  123.3 16.0 %collective-permute-start.2 = (s32[]{:T(128)}, s32[]{:T(128)}, u32[]{:S(2)}, u32[]{:S(2)}) collective-permute-start(s32[]{:T(128)} %get-tuple-element.59), channel_id=1, source_target_pairs={{0,32},{32,64},{64,96},{96,0},{1,33},{33,65},{65,97},{97,1},{2,34}... | collective-permute-start | bytes 20 | tf_op jit(solution)/shard_map/ppermute | solution.py:335
  125.0 15.6 %collective-permute-start.3 = (s32[]{:T(128)}, s32[]{:T(128)}, u32[]{:S(2)}, u32[]{:S(2)}) collective-permute-start(s32[]{:T(128)} %get-tuple-element.59), channel_id=1, source_target_pairs={{0,64},{32,96},{64,0},{96,32},{1,65},{33,97},{65,1},{97,33},{2,66}... | collective-permute-start | bytes 20 | tf_op jit(solution)/shard_map/ppermute | solution.py:335
  126.6 14.6 %collective-permute-start.4 = (s32[]{:T(128)}, s32[]{:T(128)}, u32[]{:S(2)}, u32[]{:S(2)}) collective-permute-start(s32[]{:T(128)} %get-tuple-element.59), channel_id=1, source_target_pairs={{0,96},{32,0},{64,32},{96,64},{1,97},{33,1},{65,33},{97,65},{2,98}... | collective-permute-start | bytes 20 | tf_op jit(solution)/shard_map/ppermute | solution.py:335
  191.6 58.0 %copy-start.5 = (bf16[8,512,128]{2,1,0:T(8,128)(2,1)S(1)}, bf16[8,512,128]{2,1,0:T(8,128)(2,1)}, u32[]{:S(2)}) copy-start(bf16[8,512,128]{2,1,0:T(8,128)(2,1)} %copy-done.4) | copy-start | bytes 3145732
  237.5 12.1 %copy-start.2 = (bf16[32,512,128]{2,1,0:T(8,128)(2,1)S(1)}, bf16[32,512,128]{2,1,0:T(8,128)(2,1)}, u32[]{:S(2)}) copy-start(bf16[32,512,128]{2,1,0:T(8,128)(2,1)} %own.3) | copy-start | bytes 12582916
  249.6 1.0 copy-start.6
Sparse Core Ops, SparseCore 0:
  20.9 168.1 all-gather.1

commit v2 on v1

--- a/solution.py
+++ b/solution.py
@@ -7,13 +7,18 @@
 from jax.experimental.pallas import tpu as pltpu
 from jax.sharding import PartitionSpec as P
 
-VMEM_LIMIT = 48 * 1024 * 1024
+VMEM_LIMIT = 58 * 1024 * 1024
 DEPTH = 8
+GROUPS = 4
 NOTE = 16
 
 
 def any_spec():
     return pl.BlockSpec(memory_space=pl.ANY)
+
+
+def hbm_spec():
+    return pl.BlockSpec(memory_space=pltpu.HBM)
 
 
 def smem_spec():
@@ -66,9 +71,9 @@
     shape = (count, blocks.shape[1] + NOTE, blocks.shape[2])
     return pl.pallas_call(
         order_kernel,
-        out_shape=jax.ShapeDtypeStruct(shape, blocks.dtype),
+        out_shape=pltpu.HBM(shape, blocks.dtype),
         in_specs=[smem_spec(), pl.BlockSpec(memory_space=pltpu.VMEM), any_spec()],
-        out_specs=any_spec(),
+        out_specs=hbm_spec(),
         scratch_shapes=[
             pltpu.VMEM(shape, blocks.dtype),
             pltpu.SemaphoreType.DMA((2, count)),
@@ -297,6 +302,160 @@
     )(plan, *([total] if has_total else []), received, weights)
 
 
+def pack_kernel(first_row, plan, weights, out, target, sems, out_sems):
+    sources, depth_k, wide = target.shape
+    cells = wide // 2
+    rows = pl.ds(first_row, depth_k)
+
+    def copies(q):
+        return [
+            pltpu.make_async_copy(
+                weights.at[lax.shift_right_logical(plan[(1 + i) * sources + q], 3), rows],
+                target.at[q, :, pl.ds(i * cells, cells)],
+                sems.at[i, q],
+            )
+            for i in range(2)
+        ]
+
+    def start(q, carry):
+        for copy in copies(q):
+            copy.start()
+        return carry
+
+    def end(q, carry):
+        for copy in copies(q):
+            copy.wait()
+
+        @pl.when(plan[q] == 0)
+        def dead():
+            target[q] = jnp.zeros_like(target[q])
+
+        store(q).start()
+        return carry
+
+    def store(q):
+        return pltpu.make_async_copy(target.at[q], out.at[q], out_sems.at[q])
+
+    def finish(q, carry):
+        store(q).wait()
+        return carry
+
+    lax.fori_loop(0, sources, start, 0)
+    lax.fori_loop(0, sources, end, 0)
+    lax.fori_loop(0, sources, finish, 0)
+
+
+def pack(plan, weights, first_row, depth_k):
+    sources = plan.shape[0] // 3
+    cells = weights.shape[2]
+    return pl.pallas_call(
+        functools.partial(pack_kernel, first_row),
+        out_shape=pltpu.HBM((sources, depth_k, 2 * cells), weights.dtype),
+        in_specs=[smem_spec(), hbm_spec()],
+        out_specs=hbm_spec(),
+        scratch_shapes=[
+            pltpu.VMEM((sources, depth_k, 2 * cells), weights.dtype),
+            pltpu.SemaphoreType.DMA((2, sources)),
+            pltpu.SemaphoreType.DMA((sources,)),
+        ],
+        compiler_params=pltpu.CompilerParams(vmem_limit_bytes=VMEM_LIMIT),
+        cost_estimate=pl.CostEstimate(
+            flops=0, transcendentals=0, bytes_accessed=8 * sources * depth_k * cells
+        ),
+        name="pack",
+    )(plan, weights)
+
+
+def packed_kernel(has_total, plan, *refs):
+    if has_total:
+        total_in, tiles, received, out, total, held, fields, rounded, sems, total_sems = refs
+    else:
+        tiles, received, out, total, held, fields, rounded, sems, total_sems = refs
+    sources, columns, depth_k = received.shape
+    oceans, unused, cells = out.shape
+    group = sources // GROUPS
+
+    def fetch(g):
+        some = pl.ds(g * group, group)
+        return (
+            pltpu.make_async_copy(received.at[some], fields.at[some], sems.at[0, g]),
+            pltpu.make_async_copy(tiles.at[some], held.at[some], sems.at[1, g]),
+        )
+
+    live = lax.fori_loop(0, sources, lambda q, seen: seen + plan[q], 0)
+    if has_total:
+        earlier = pltpu.make_async_copy(total_in, total, total_sems.at[0])
+        earlier.start()
+
+    @pl.when(live > 0)
+    def begin():
+        for g in range(GROUPS):
+            for copy in fetch(g):
+                copy.start()
+
+    if has_total:
+        earlier.wait()
+    else:
+        total[...] = jnp.zeros_like(total)
+    part = min(columns, 256)
+
+    def add(q, carry):
+        first_ocean = plan[sources + q] & 7
+        second_ocean = plan[2 * sources + q] & 7
+        for begin in range(0, columns, part):
+            rows = pl.ds(begin, part)
+            product = jnp.dot(fields[q, rows, :], held[q], preferred_element_type=jnp.float32)
+            total[first_ocean, rows, :] += product[:, :cells]
+            total[second_ocean, rows, :] += product[:, cells:]
+        return carry
+
+    @pl.when(live > 0)
+    def work():
+        for g in range(GROUPS):
+            for copy in fetch(g):
+                copy.wait()
+            lax.fori_loop(g * group, (g + 1) * group, add, 0, unroll=group)
+
+    stores = []
+    for o in range(oceans):
+        source = total
+        if out.dtype != total.dtype:
+            rounded[o] = total[o].astype(out.dtype)
+            source = rounded
+        store = pltpu.make_async_copy(source.at[o], out.at[o], total_sems.at[o])
+        store.start()
+        stores.append(store)
+    for store in stores:
+        store.wait()
+
+
+def remap_packed(plan, total, tiles, received, ocean_count, dtype):
+    sources, columns, depth_k = received.shape
+    shape = (ocean_count, columns, tiles.shape[2] // 2)
+    has_total = total is not None
+    return pl.pallas_call(
+        functools.partial(packed_kernel, has_total),
+        out_shape=pltpu.HBM(shape, dtype),
+        in_specs=[smem_spec()] + [hbm_spec()] * (2 + has_total),
+        out_specs=hbm_spec(),
+        scratch_shapes=[
+            pltpu.VMEM(shape, jnp.float32),
+            pltpu.VMEM(tiles.shape, tiles.dtype),
+            pltpu.VMEM(received.shape, received.dtype),
+            pltpu.VMEM(shape, jnp.bfloat16),
+            pltpu.SemaphoreType.DMA((2, GROUPS)),
+            pltpu.SemaphoreType.DMA((ocean_count,)),
+        ],
+        compiler_params=pltpu.CompilerParams(vmem_limit_bytes=VMEM_LIMIT),
+        cost_estimate=pl.CostEstimate(
+            flops=4 * sources * columns * depth_k * shape[2],
+            transcendentals=0,
+            bytes_accessed=2 * sources * columns * depth_k,
+        ),
+        name="remap_packed",
+    )(plan, *([total] if has_total else []), tiles, received)
+
+
 def body(atm_fields, neighbours, send_slots, send_counts, tile_weights, tile_rows, tile_cols):
     block_count, column_count, cell_count = atm_fields.shape
     peers = lax.axis_size("gy")
@@ -358,15 +517,16 @@
     total = add(plan_first, values, None, 0)
     total = add(plan_spare, spares, total, 0)
 
-    def finish(total):
-        return add(plan_first, slopes, total, cell_count, final=True)
+    tiles = pack(plan_first, tile_weights, cell_count, 2 * cell_count)
+    done = remap_packed(plan_first, total, tiles, slopes, ocean_count, jnp.bfloat16)
 
     def with_rest(total, unused):
         rest_slopes = gradients(slots[:, 1], near, low, atm_fields, high)
         total = add(plan_rest, exchange(in_order(atm_fields, slots[:, 1], note)), total, 0)
-        return finish(add(plan_rest, exchange(rest_slopes), total, cell_count))
-
-    return lax.cond(most > 1, with_rest, lambda unused, done: done, total, finish(total))
+        total = add(plan_rest, exchange(rest_slopes), total, cell_count)
+        return add(plan_first, slopes, total, cell_count, final=True)
+
+    return lax.cond(most > 1, with_rest, lambda unused, done: done, total, done)
 
 
 def solution(mesh):

time: 256 us -> 251 us (0.980); the launches traced: 257 us -> 248 us
  waiting for transfers between devices: 147 us -> 139 us
    all_to_all x2, waiting for transfers between devices: 99.6 us -> 59.6 us  [exchange(): return lax.all_to_all(blocks, 'gy', split_axis=0, concat_axis=0, tiled=True)]
    all_gather x1, waiting for transfers between devices: 47.2 us -> 79.4 us  [body(): lax.all_gather(one_payload(where, low, atm_fields, high), 'gy', axis=0, t...]
    pallas_call x1 -> x3, Pallas kernels: 8.02 us -> 19.2 us  [the longest x1 8.8 us: remap_packed(): pl.pallas_call(functools.partial(packed_kernel, has_total), out_shape=plt...]
    pallas_call x3 -> x2, Pallas kernels: 24.1 us -> 13.9 us  [remap(): pl.pallas_call(kernel, out_shape=jax.ShapeDtypeStruct(shape, jnp.bfloat16...]
    unnamed x20 -> x12, local copies, waits for them, and re-layouts: 3.14 us -> 0.2 us
  transfers between devices with their start and end apart: 8 -> 8, of which waited for: 3 -> 3; matrix products, arithmetic and copies ran while one was open for 3% -> 3% of each run, Pallas kernels for 10% -> 13%
where the time goes in v2:
time: 251 us; the launch traced here: 248 us
  waiting for transfers between devices  139 us (55%)
  Pallas kernels  42.9 us (17%)
  starting transfers between devices  36 us (14%)
  between operations  19.1 us (8%)
  other arithmetic  6.18 us (2%)
  local copies, waits for them, and re-layouts  5.17 us (2%)
    all_gather x1, waiting for transfers between devices, body(): lax.all_gather(one_payload(where, low, atm_fields, high), 'gy', axis=0, t...  79.4 us
    all_to_all x2, waiting for transfers between devices, exchange(): return lax.all_to_all(blocks, 'gy', split_axis=0, concat_axis=0, tiled=True)  59.6 us
    all_to_all x2, starting transfers between devices, exchange(): return lax.all_to_all(blocks, 'gy', split_axis=0, concat_axis=0, tiled=True)  27.1 us
    pallas_call x2, Pallas kernels, remap(): pl.pallas_call(kernel, out_shape=jax.ShapeDtypeStruct(shape, jnp.bfloat16...  13.9 us
    pallas_call x1, Pallas kernels, remap_packed(): pl.pallas_call(functools.partial(packed_kernel, has_total), out_shape=plt...  8.8 us
    pallas_call x1, Pallas kernels, gradients(): pl.pallas_call(gradient_kernel, out_shape=jax.ShapeDtypeStruct((steps, co...  7.04 us
    ppermute x3, starting transfers between devices, body(): lax.ppermute(most, 'gx', [(i, (i + step) % planes) for i in range(planes)])  6.19 us
    pallas_call x1, Pallas kernels, pack(): pl.pallas_call(functools.partial(pack_kernel, first_row), out_shape=pltpu...  5.47 us
  transfers between devices with their start and end apart: 8, of which 3 were waited for; matrix products, arithmetic and copies ran while one was open for 3% of the time, Pallas kernels for 13%

profile of v2, /device:TPU:0, one launch (start us, length us, event | category | flops | bytes accessed | tf_op | source)
XLA Modules:
  0.0 248.4 jit_solution(2287505492848636204)
XLA Ops:
  6.5 2.7 %fusion.3 = (bf16[8,512,128]{2,1,0:T(8,128)(2,1)S(1)}, bf16[8,512,128]{2,1,0:T(8,128)(2,1)}) fusion(bf16[32,512,128]{2,1,0:T(8,128)(2,1)} %own.3), kind=kLoop, calls=%fused_computation.30 | loop fusion | bytes 4194304 | tf_op jit(solution)/shard_map/slice | solution.py:34
  9.2 1.5 collective-permute-start
  10.7 1.3 collective-permute-start.1
  12.0 0.7 fusion.1
  12.8 0.1 compare_reduce_fusion
  12.9 1.3 fusion.2
  16.5 0.7 broadcast_subtract_fusion
  17.2 0.2 dynamic-slice_reduce_fusion
  17.4 0.6 pad_add_fusion.1.where
  18.0 2.7 %payload.1 = bf16[1,512,384]{2,1,0:T(8,128)(2,1)} custom-call(s32[5]{0:T(128)} %pad_add_fusion.1.where, bf16[8,512,128]{2,1,0:T(8,128)(2,1)S(1)} %collective-permute-done.low, bf16[32,512,128]{2,1,0:T(8,128)(2,1)} %own.3, bf16[8,512,128]{2,1,0:T(8,128)(2,1)S(1)} %collective-permute-done.1.high), custom_call_target="tpu_custom_call" | custom-call | bytes 1048576 | tf_op jit(solution)/shard_map/payload/pallas_call | solution.py:188
  20.8 0.5 slice.60
  22.2 0.6 slice_bitcast_fusion.1.slots
  22.8 5.0 %order.3 = bf16[32,528,128]{2,1,0:T(8,128)(2,1)} custom-call(s32[32]{0:T(128)} %slice_bitcast_fusion.1.slots, bf16[32,128]{1,0:T(8,128)(2,1)S(1)} %pad.4.note, bf16[32,512,128]{2,1,0:T(8,128)(2,1)} %own.3), custom_call_target="tpu_custom_call" | custom-call | bytes 8650752 | tf_op jit(solution)/shard_map/order/pallas_call | solution.py:72
  27.8 22.1 %all-to-all-start.2 = ((bf16[32,528,128]{2,1,0:T(8,128)(2,1)}), bf16[32,528,128]{2,1,0:T(8,128)(2,1)}, u32[]{:S(2)}, u32[]{:S(2)}) async-start(bf16[32,528,128]{2,1,0:T(8,128)(2,1)} %order.3), calls=%async_computation.2 | async-start | bytes 8650752 | tf_op jit(solution)/shard_map/all_to_all | solution.py:470
  50.1 7.0 %gradients.3 = bf16[32,512,256]{2,1,0:T(8,128)(2,1)} custom-call(s32[32]{0:T(128)} %slice_bitcast_fusion.1.slots, s32[128]{0:T(128)S(1)} %reshape.58.near, bf16[8,512,128]{2,1,0:T(8,128)(2,1)S(1)} %collective-permute-done.low, bf16[32,512,128]{2,1,0:T(8,128)(2,1)} %own.3, bf16[8,512,128]{2,1,0:T(8,128)(2,1)S(1)} %collective-permute-done.1.high), custom_call_target="tpu_custom_call" | custom-call | flops 8388608 | bytes 16777216 | tf_op jit(solution)/shard_map/gradients/pallas_call | solution.py:134
  57.2 51.8 %all-to-all-done.2.refs_0_ = bf16[32,528,128]{2,1,0:T(8,128)(2,1)} async-done(((bf16[32,528,128]{2,1,0:T(8,128)(2,1)}), bf16[32,528,128]{2,1,0:T(8,128)(2,1)}, u32[]{:S(2)}, u32[]{:S(2)}) %all-to-all-start.2) | async-done | bytes 4325408 | tf_op jit(solution)/shard_map/all_to_all | solution.py:470
  109.0 5.0 %all-to-all-start.3 = ((bf16[32,512,256]{2,1,0:T(8,128)(2,1)}), bf16[32,512,256]{2,1,0:T(8,128)(2,1)}, u32[]{:S(2)}, u32[]{:S(2)}) async-start(bf16[32,512,256]{2,1,0:T(8,128)(2,1)} %gradients.3), calls=%async_computation.3 | async-start | bytes 16777216 | tf_op jit(solution)/shard_map/all_to_all | solution.py:470
  114.0 0.1 select_reduce_fusion.1
  114.4 0.2 slice_reduce_fusion
  114.6 0.9 slice_convert_fusion
  115.6 0.7 fusion.4
  116.3 1.6 collective-permute-start.2
  117.9 2.7 %collective-permute-start.3 = (s32[]{:T(128)}, s32[]{:T(128)}, u32[]{:S(2)}, u32[]{:S(2)}) collective-permute-start(s32[]{:T(128)} %get-tuple-element.59), channel_id=1, source_target_pairs={{0,64},{32,96},{64,0},{96,32},{1,65},{33,97},{65,1},{97,33},{2,66}... | collective-permute-start | bytes 20 | tf_op jit(solution)/shard_map/ppermute | solution.py:494
  120.6 1.8 collective-permute-start.4
  122.8 5.5 %pack.1.refs_1_ = bf16[32,256,256]{2,1,0:T(8,128)(2,1)} custom-call(s32[96]{0:T(128)S(1)} %pad_add_fusion.plan, bf16[128,384,128]{2,1,0:T(8,128)(2,1)} %weights.1), custom_call_target="tpu_custom_call" | custom-call | bytes 8388608 | tf_op jit(solution)/shard_map/pack/pallas_call | solution.py:351
  128.3 11.1 %remap.8.refs_0_ = f32[8,512,128]{2,1,0:T(8,128)} custom-call(s32[96]{0:T(128)S(1)} %pad_add_fusion.plan, bf16[32,528,128]{2,1,0:T(8,128)(2,1)} %all-to-all-done.2.refs_0_, bf16[128,384,128]{2,1,0:T(8,128)(2,1)} %weights.1), custom_call_target="tpu_custom_call" | custom-call | flops 1073741824 | bytes 8388608 | tf_op jit(solution)/shard_map/remap/pallas_call | solution.py:282
  139.4 0.1 convert_reduce_fusion
  139.5 0.7 add_add_fusion.1
  142.8 79.4 %all-gather.2.cloned.1.call-done.refs_1_ = bf16[32,512,384]{2,1,0:T(8,128)(2,1)} async-done(((bf16[1,512,384]{2,1,0:T(8,128)(2,1)}), bf16[32,512,384]{2,1,0:T(8,128)(2,1)}) %all-gather.2.cloned.1.call-update) | async-done | bytes 12582928 | tf_op jit(solution)/shard_map/all_gather | solution.py:482
  222.1 2.8 %remap.9.refs_0_ = f32[8,512,128]{2,1,0:T(8,128)S(1)} custom-call(s32[96]{0:T(128)} %get-tuple-element.61.plan, f32[8,512,128]{2,1,0:T(8,128)} %remap.8.refs_0_, bf16[32,512,384]{2,1,0:T(8,128)(2,1)} %all-gather.2.cloned.1.call-done.refs_1_, bf16[128,384,128]{2,1,0:T(8,128)(2,1)} %weights.1), custom_call_target="tpu_custom_call" | custom-call | flops 3221225472 | bytes 25165824 | tf_op jit(solution)/shard_map/remap/pallas_call | solution.py:282
  224.9 7.8 %all-to-all-done.3.refs_2_ = bf16[32,512,256]{2,1,0:T(8,128)(2,1)} async-done(((bf16[32,512,256]{2,1,0:T(8,128)(2,1)}), bf16[32,512,256]{2,1,0:T(8,128)(2,1)}, u32[]{:S(2)}, u32[]{:S(2)}) %all-to-all-start.3) | async-done | bytes 8388640 | tf_op jit(solution)/shard_map/all_to_all | solution.py:470
  232.7 8.8 %remap_packed.1 = bf16[8,512,128]{2,1,0:T(8,128)(2,1)} custom-call(s32[96]{0:T(128)S(1)} %pad_add_fusion.plan, f32[8,512,128]{2,1,0:T(8,128)S(1)} %remap.9.refs_0_, bf16[32,256,256]{2,1,0:T(8,128)(2,1)} %pack.1.refs_1_, bf16[32,512,256]{2,1,0:T(8,128)(2,1)} %all-to-all-done.3.refs_2_), custom_call_target="tpu_custom_call" | custom-call | flops 2147483648 | bytes 8388608 | tf_op jit(solution)/shard_map/remap_packed/pallas_call | solution.py:436
  (36 shorter events, 1.3 us)
Async XLA Ops:
  6.5 215.6 %all-gather.2.cloned.1.call-start = ((), (), s32[]{:S(2)}) async-start(), calls=%async_computation.4 | async-start | bytes 12976128 | tf_op jit(solution)/shard_map/all_gather | solution.py:482
  9.2 12.7 %copy-start.1 = (s32[1,32]{1,0:T(1,128)S(1)}, s32[1,32]{1,0:T(1,128)}, u32[]{:S(2)}) copy-start(s32[1,32]{1,0:T(1,128)} %param.12) | copy-start | bytes 388
  9.2 13.0 %copy-start.3 = (s32[1,32,2]{1,2,0:T(2,128)S(1)}, s32[1,32,2]{1,2,0:T(2,128)}, u32[]{:S(2)}) copy-start(s32[1,32,2]{1,2,0:T(2,128)} %param.11) | copy-start | bytes 772
  9.2 8.7 %collective-permute-start = (bf16[8,512,128]{2,1,0:T(8,128)(2,1)}, bf16[8,512,128]{2,1,0:T(8,128)(2,1)S(1)}, u32[]{:S(2)}, u32[]{:S(2)}) collective-permute-start(bf16[8,512,128]{2,1,0:T(8,128)(2,1)} %get-tuple-element.56), channel_id=1, source_target_pairs={{0,1},{1,2},{2,3},{3,4},{4,5},{5,6},{6,7},{7,8},{8,9},{9,10},{10,1... | collective-permute-start | bytes 3145736 | tf_op jit(solution)/shard_map/ppermute | solution.py:33
  10.7 7.3 %collective-permute-start.1 = (bf16[8,512,128]{2,1,0:T(8,128)(2,1)S(1)}, bf16[8,512,128]{2,1,0:T(8,128)(2,1)S(1)}, u32[]{:S(2)}, u32[]{:S(2)}) collective-permute-start(bf16[8,512,128]{2,1,0:T(8,128)(2,1)S(1)} %get-tuple-element.55), channel_id=1, source_target_pairs={{1,0},{2,1},{3,2},{4,3},{5,4},{6,5},{7,6},{8,7},{9,8},{10,9},{11,1... | collective-permute-start | bytes 3145736 | tf_op jit(solution)/shard_map/ppermute | solution.py:34
  18.0 32.1 %copy-start = (bf16[8,512,128]{2,1,0:T(8,128)(2,1)}, bf16[8,512,128]{2,1,0:T(8,128)(2,1)S(1)}, u32[]{:S(2)}) copy-start(bf16[8,512,128]{2,1,0:T(8,128)(2,1)S(1)} %collective-permute-done.1.high) | copy-start | bytes 3145732
  27.8 81.2 %all-to-all-start.2 = ((bf16[32,528,128]{2,1,0:T(8,128)(2,1)}), bf16[32,528,128]{2,1,0:T(8,128)(2,1)}, u32[]{:S(2)}, u32[]{:S(2)}) async-start(bf16[32,528,128]{2,1,0:T(8,128)(2,1)} %order.3), calls=%async_computation.2 | async-start | bytes 8650752 | tf_op jit(solution)/shard_map/all_to_all | solution.py:470
  57.1 56.9 %copy-start.4 = (s32[128]{0:T(128)S(1)}, s32[128]{0:T(128)}, u32[]{:S(2)}) copy-start(s32[128]{0:T(128)} %param.14) | copy-start | bytes 1540
  57.2 56.9 %copy-start.2 = (s32[128]{0:T(128)S(1)}, s32[128]{0:T(128)}, u32[]{:S(2)}) copy-start(s32[128]{0:T(128)} %param.15) | copy-start | bytes 1540
  109.0 123.7 %all-to-all-start.3 = ((bf16[32,512,256]{2,1,0:T(8,128)(2,1)}), bf16[32,512,256]{2,1,0:T(8,128)(2,1)}, u32[]{:S(2)}, u32[]{:S(2)}) async-start(bf16[32,512,256]{2,1,0:T(8,128)(2,1)} %gradients.3), calls=%async_computation.3 | async-start | bytes 16777216 | tf_op jit(solution)/shard_map/all_to_all | solution.py:470
  116.3 23.9 %collective-permute-start.2 = (s32[]{:T(128)}, s32[]{:T(128)}, u32[]{:S(2)}, u32[]{:S(2)}) collective-permute-start(s32[]{:T(128)} %get-tuple-element.59), channel_id=1, source_target_pairs={{0,32},{32,64},{64,96},{96,0},{1,33},{33,65},{65,97},{97,1},{2,34}... | collective-permute-start | bytes 20 | tf_op jit(solution)/shard_map/ppermute | solution.py:494
  117.9 23.5 %collective-permute-start.3 = (s32[]{:T(128)}, s32[]{:T(128)}, u32[]{:S(2)}, u32[]{:S(2)}) collective-permute-start(s32[]{:T(128)} %get-tuple-element.59), channel_id=1, source_target_pairs={{0,64},{32,96},{64,0},{96,32},{1,65},{33,97},{65,1},{97,33},{2,66}... | collective-permute-start | bytes 20 | tf_op jit(solution)/shard_map/ppermute | solution.py:494
  120.6 21.5 %collective-permute-start.4 = (s32[]{:T(128)}, s32[]{:T(128)}, u32[]{:S(2)}, u32[]{:S(2)}) collective-permute-start(s32[]{:T(128)} %get-tuple-element.59), channel_id=1, source_target_pairs={{0,96},{32,0},{64,32},{96,64},{1,97},{33,1},{65,33},{97,65},{2,98}... | collective-permute-start | bytes 20 | tf_op jit(solution)/shard_map/ppermute | solution.py:494
Sparse Core Ops, SparseCore 0:
  20.9 201.2 all-gather.1

commit v3 on v2

--- a/solution.py
+++ b/solution.py
@@ -9,7 +9,8 @@
 
 VMEM_LIMIT = 58 * 1024 * 1024
 DEPTH = 8
-GROUPS = 4
+GROUP_ENDS = (0, 1, 4, 8, 12, 16)
+GROUPS = len(GROUP_ENDS) - 1
 NOTE = 16
 
 
@@ -373,10 +374,10 @@
         tiles, received, out, total, held, fields, rounded, sems, total_sems = refs
     sources, columns, depth_k = received.shape
     oceans, unused, cells = out.shape
-    group = sources // GROUPS
+    ends = [end * sources // 16 for end in GROUP_ENDS]
 
     def fetch(g):
-        some = pl.ds(g * group, group)
+        some = pl.ds(ends[g], ends[g + 1] - ends[g])
         return (
             pltpu.make_async_copy(received.at[some], fields.at[some], sems.at[0, g]),
             pltpu.make_async_copy(tiles.at[some], held.at[some], sems.at[1, g]),
@@ -414,7 +415,7 @@
         for g in range(GROUPS):
             for copy in fetch(g):
                 copy.wait()
-            lax.fori_loop(g * group, (g + 1) * group, add, 0, unroll=group)
+            lax.fori_loop(ends[g], ends[g + 1], add, 0, unroll=ends[g + 1] - ends[g])
 
     stores = []
     for o in range(oceans):

time: 251 us -> 252 us (level)
    all_to_all x2, waiting for transfers between devices: 59.6 us -> 75.4 us  [exchange(): return lax.all_to_all(blocks, 'gy', split_axis=0, concat_axis=0, tiled=True)]
    all_gather x1, waiting for transfers between devices: 79.4 us -> 64.9 us  [body(): lax.all_gather(one_payload(where, low, atm_fields, high), 'gy', axis=0, t...]
where the time goes in v3:
time: 252 us; the launch traced here: 249 us
  waiting for transfers between devices  140 us (56%)
  Pallas kernels  42.7 us (17%)
  starting transfers between devices  35.3 us (14%)
  between operations  19.1 us (8%)
  other arithmetic  6.15 us (2%)
  local copies, waits for them, and re-layouts  5.17 us (2%)
    all_to_all x2, waiting for transfers between devices, exchange(): return lax.all_to_all(blocks, 'gy', split_axis=0, concat_axis=0, tiled=True)  75.4 us
    all_gather x1, waiting for transfers between devices, body(): lax.all_gather(one_payload(where, low, atm_fields, high), 'gy', axis=0, t...  64.9 us
    all_to_all x2, starting transfers between devices, exchange(): return lax.all_to_all(blocks, 'gy', split_axis=0, concat_axis=0, tiled=True)  26.9 us
    pallas_call x2, Pallas kernels, remap(): pl.pallas_call(kernel, out_shape=jax.ShapeDtypeStruct(shape, jnp.bfloat16...  13.7 us
    pallas_call x1, Pallas kernels, remap_packed(): pl.pallas_call(functools.partial(packed_kernel, has_total), out_shape=plt...  8.51 us
    pallas_call x1, Pallas kernels, gradients(): pl.pallas_call(gradient_kernel, out_shape=jax.ShapeDtypeStruct((steps, co...  7.04 us
    ppermute x3, starting transfers between devices, body(): lax.ppermute(most, 'gx', [(i, (i + step) % planes) for i in range(planes)])  5.67 us
    pallas_call x1, Pallas kernels, pack(): pl.pallas_call(functools.partial(pack_kernel, first_row), out_shape=pltpu...  5.44 us
  transfers between devices with their start and end apart: 8, of which 3 were waited for; matrix products, arithmetic and copies ran while one was open for 3% of the time, Pallas kernels for 13%

profile of v3, /device:TPU:0, one launch (start us, length us, event | category | flops | bytes accessed | tf_op | source)
XLA Modules:
  0.0 248.7 jit_solution(926058341491432683)
XLA Ops:
  6.5 2.7 %fusion.3 = (bf16[8,512,128]{2,1,0:T(8,128)(2,1)S(1)}, bf16[8,512,128]{2,1,0:T(8,128)(2,1)}) fusion(bf16[32,512,128]{2,1,0:T(8,128)(2,1)} %own.3), kind=kLoop, calls=%fused_computation.30 | loop fusion | bytes 4194304 | tf_op jit(solution)/shard_map/slice | solution.py:35
  9.2 1.5 collective-permute-start
  10.7 1.3 collective-permute-start.1
  12.0 0.7 fusion.1
  12.8 0.1 compare_reduce_fusion
  12.9 1.3 fusion.2
  16.5 0.7 broadcast_subtract_fusion
  17.2 0.2 dynamic-slice_reduce_fusion
  17.4 0.6 pad_add_fusion.1.where
  18.0 2.7 %payload.1 = bf16[1,512,384]{2,1,0:T(8,128)(2,1)} custom-call(s32[5]{0:T(128)} %pad_add_fusion.1.where, bf16[8,512,128]{2,1,0:T(8,128)(2,1)S(1)} %collective-permute-done.low, bf16[32,512,128]{2,1,0:T(8,128)(2,1)} %own.3, bf16[8,512,128]{2,1,0:T(8,128)(2,1)S(1)} %collective-permute-done.1.high), custom_call_target="tpu_custom_call" | custom-call | bytes 1048576 | tf_op jit(solution)/shard_map/payload/pallas_call | solution.py:189
  20.8 0.5 slice.60
  22.2 0.6 slice_bitcast_fusion.1.slots
  22.8 5.2 %order.3 = bf16[32,528,128]{2,1,0:T(8,128)(2,1)} custom-call(s32[32]{0:T(128)} %slice_bitcast_fusion.1.slots, bf16[32,128]{1,0:T(8,128)(2,1)S(1)} %pad.4.note, bf16[32,512,128]{2,1,0:T(8,128)(2,1)} %own.3), custom_call_target="tpu_custom_call" | custom-call | bytes 8650752 | tf_op jit(solution)/shard_map/order/pallas_call | solution.py:73
  28.1 21.9 %all-to-all-start.2 = ((bf16[32,528,128]{2,1,0:T(8,128)(2,1)}), bf16[32,528,128]{2,1,0:T(8,128)(2,1)}, u32[]{:S(2)}, u32[]{:S(2)}) async-start(bf16[32,528,128]{2,1,0:T(8,128)(2,1)} %order.3), calls=%async_computation.2 | async-start | bytes 8650752 | tf_op jit(solution)/shard_map/all_to_all | solution.py:471
  50.2 7.0 %gradients.3 = bf16[32,512,256]{2,1,0:T(8,128)(2,1)} custom-call(s32[32]{0:T(128)} %slice_bitcast_fusion.1.slots, s32[128]{0:T(128)S(1)} %reshape.58.near, bf16[8,512,128]{2,1,0:T(8,128)(2,1)S(1)} %collective-permute-done.low, bf16[32,512,128]{2,1,0:T(8,128)(2,1)} %own.3, bf16[8,512,128]{2,1,0:T(8,128)(2,1)S(1)} %collective-permute-done.1.high), custom_call_target="tpu_custom_call" | custom-call | flops 8388608 | bytes 16777216 | tf_op jit(solution)/shard_map/gradients/pallas_call | solution.py:135
  57.3 53.7 %all-to-all-done.2.refs_0_ = bf16[32,528,128]{2,1,0:T(8,128)(2,1)} async-done(((bf16[32,528,128]{2,1,0:T(8,128)(2,1)}), bf16[32,528,128]{2,1,0:T(8,128)(2,1)}, u32[]{:S(2)}, u32[]{:S(2)}) %all-to-all-start.2) | async-done | bytes 4325408 | tf_op jit(solution)/shard_map/all_to_all | solution.py:471
  110.9 5.0 %all-to-all-start.3 = ((bf16[32,512,256]{2,1,0:T(8,128)(2,1)}), bf16[32,512,256]{2,1,0:T(8,128)(2,1)}, u32[]{:S(2)}, u32[]{:S(2)}) async-start(bf16[32,512,256]{2,1,0:T(8,128)(2,1)} %gradients.3), calls=%async_computation.3 | async-start | bytes 16777216 | tf_op jit(solution)/shard_map/all_to_all | solution.py:471
  116.0 0.1 select_reduce_fusion.1
  116.3 0.2 slice_reduce_fusion
  116.5 0.9 slice_convert_fusion
  117.5 0.7 fusion.4
  118.2 2.1 collective-permute-start.2
  120.2 1.9 collective-permute-start.3
  122.1 1.7 collective-permute-start.4
  124.2 5.4 %pack.1.refs_1_ = bf16[32,256,256]{2,1,0:T(8,128)(2,1)} custom-call(s32[96]{0:T(128)S(1)} %pad_add_fusion.plan, bf16[128,384,128]{2,1,0:T(8,128)(2,1)} %weights.1), custom_call_target="tpu_custom_call" | custom-call | bytes 8388608 | tf_op jit(solution)/shard_map/pack/pallas_call | solution.py:352
  129.6 10.9 %remap.8.refs_0_ = f32[8,512,128]{2,1,0:T(8,128)} custom-call(s32[96]{0:T(128)S(1)} %pad_add_fusion.plan, bf16[32,528,128]{2,1,0:T(8,128)(2,1)} %all-to-all-done.2.refs_0_, bf16[128,384,128]{2,1,0:T(8,128)(2,1)} %weights.1), custom_call_target="tpu_custom_call" | custom-call | flops 1073741824 | bytes 8388608 | tf_op jit(solution)/shard_map/remap/pallas_call | solution.py:283
  140.5 0.1 convert_reduce_fusion
  140.6 0.7 add_add_fusion.1
  143.9 64.9 %all-gather.2.cloned.1.call-done.refs_1_ = bf16[32,512,384]{2,1,0:T(8,128)(2,1)} async-done(((bf16[1,512,384]{2,1,0:T(8,128)(2,1)}), bf16[32,512,384]{2,1,0:T(8,128)(2,1)}) %all-gather.2.cloned.1.call-update) | async-done | bytes 12582928 | tf_op jit(solution)/shard_map/all_gather | solution.py:483
  208.8 2.8 %remap.9.refs_0_ = f32[8,512,128]{2,1,0:T(8,128)S(1)} custom-call(s32[96]{0:T(128)} %get-tuple-element.61.plan, f32[8,512,128]{2,1,0:T(8,128)} %remap.8.refs_0_, bf16[32,512,384]{2,1,0:T(8,128)(2,1)} %all-gather.2.cloned.1.call-done.refs_1_, bf16[128,384,128]{2,1,0:T(8,128)(2,1)} %weights.1), custom_call_target="tpu_custom_call" | custom-call | flops 3221225472 | bytes 25165824 | tf_op jit(solution)/shard_map/remap/pallas_call | solution.py:283
  211.6 21.7 %all-to-all-done.3.refs_2_ = bf16[32,512,256]{2,1,0:T(8,128)(2,1)} async-done(((bf16[32,512,256]{2,1,0:T(8,128)(2,1)}), bf16[32,512,256]{2,1,0:T(8,128)(2,1)}, u32[]{:S(2)}, u32[]{:S(2)}) %all-to-all-start.3) | async-done | bytes 8388640 | tf_op jit(solution)/shard_map/all_to_all | solution.py:471
  233.3 8.5 %remap_packed.1 = bf16[8,512,128]{2,1,0:T(8,128)(2,1)} custom-call(s32[96]{0:T(128)S(1)} %pad_add_fusion.plan, f32[8,512,128]{2,1,0:T(8,128)S(1)} %remap.9.refs_0_, bf16[32,256,256]{2,1,0:T(8,128)(2,1)} %pack.1.refs_1_, bf16[32,512,256]{2,1,0:T(8,128)(2,1)} %all-to-all-done.3.refs_2_), custom_call_target="tpu_custom_call" | custom-call | flops 2147483648 | bytes 8388608 | tf_op jit(solution)/shard_map/remap_packed/pallas_call | solution.py:437
  (36 shorter events, 1.3 us)
Async XLA Ops:
  6.5 202.2 %all-gather.2.cloned.1.call-start = ((), (), s32[]{:S(2)}) async-start(), calls=%async_computation.4 | async-start | bytes 12976128 | tf_op jit(solution)/shard_map/all_gather | solution.py:483
  9.2 12.7 %copy-start.1 = (s32[1,32]{1,0:T(1,128)S(1)}, s32[1,32]{1,0:T(1,128)}, u32[]{:S(2)}) copy-start(s32[1,32]{1,0:T(1,128)} %param.12) | copy-start | bytes 388
  9.2 13.0 %copy-start.3 = (s32[1,32,2]{1,2,0:T(2,128)S(1)}, s32[1,32,2]{1,2,0:T(2,128)}, u32[]{:S(2)}) copy-start(s32[1,32,2]{1,2,0:T(2,128)} %param.11) | copy-start | bytes 772
  9.2 8.7 %collective-permute-start = (bf16[8,512,128]{2,1,0:T(8,128)(2,1)}, bf16[8,512,128]{2,1,0:T(8,128)(2,1)S(1)}, u32[]{:S(2)}, u32[]{:S(2)}) collective-permute-start(bf16[8,512,128]{2,1,0:T(8,128)(2,1)} %get-tuple-element.56), channel_id=1, source_target_pairs={{0,1},{1,2},{2,3},{3,4},{4,5},{5,6},{6,7},{7,8},{8,9},{9,10},{10,1... | collective-permute-start | bytes 3145736 | tf_op jit(solution)/shard_map/ppermute | solution.py:34
  10.7 7.3 %collective-permute-start.1 = (bf16[8,512,128]{2,1,0:T(8,128)(2,1)S(1)}, bf16[8,512,128]{2,1,0:T(8,128)(2,1)S(1)}, u32[]{:S(2)}, u32[]{:S(2)}) collective-permute-start(bf16[8,512,128]{2,1,0:T(8,128)(2,1)S(1)} %get-tuple-element.55), channel_id=1, source_target_pairs={{1,0},{2,1},{3,2},{4,3},{5,4},{6,5},{7,6},{8,7},{9,8},{10,9},{11,1... | collective-permute-start | bytes 3145736 | tf_op jit(solution)/shard_map/ppermute | solution.py:35
  18.0 32.2 %copy-start = (bf16[8,512,128]{2,1,0:T(8,128)(2,1)}, bf16[8,512,128]{2,1,0:T(8,128)(2,1)S(1)}, u32[]{:S(2)}) copy-start(bf16[8,512,128]{2,1,0:T(8,128)(2,1)S(1)} %collective-permute-done.1.high) | copy-start | bytes 3145732
  28.1 82.9 %all-to-all-start.2 = ((bf16[32,528,128]{2,1,0:T(8,128)(2,1)}), bf16[32,528,128]{2,1,0:T(8,128)(2,1)}, u32[]{:S(2)}, u32[]{:S(2)}) async-start(bf16[32,528,128]{2,1,0:T(8,128)(2,1)} %order.3), calls=%async_computation.2 | async-start | bytes 8650752 | tf_op jit(solution)/shard_map/all_to_all | solution.py:471
  57.2 58.7 %copy-start.4 = (s32[128]{0:T(128)S(1)}, s32[128]{0:T(128)}, u32[]{:S(2)}) copy-start(s32[128]{0:T(128)} %param.14) | copy-start | bytes 1540
  57.3 58.7 %copy-start.2 = (s32[128]{0:T(128)S(1)}, s32[128]{0:T(128)}, u32[]{:S(2)}) copy-start(s32[128]{0:T(128)} %param.15) | copy-start | bytes 1540
  110.9 122.4 %all-to-all-start.3 = ((bf16[32,512,256]{2,1,0:T(8,128)(2,1)}), bf16[32,512,256]{2,1,0:T(8,128)(2,1)}, u32[]{:S(2)}, u32[]{:S(2)}) async-start(bf16[32,512,256]{2,1,0:T(8,128)(2,1)} %gradients.3), calls=%async_computation.3 | async-start | bytes 16777216 | tf_op jit(solution)/shard_map/all_to_all | solution.py:471
  118.2 23.1 %collective-permute-start.2 = (s32[]{:T(128)}, s32[]{:T(128)}, u32[]{:S(2)}, u32[]{:S(2)}) collective-permute-start(s32[]{:T(128)} %get-tuple-element.59), channel_id=1, source_target_pairs={{0,32},{32,64},{64,96},{96,0},{1,33},{33,65},{65,97},{97,1},{2,34}... | collective-permute-start | bytes 20 | tf_op jit(solution)/shard_map/ppermute | solution.py:495
  120.2 22.3 %collective-permute-start.3 = (s32[]{:T(128)}, s32[]{:T(128)}, u32[]{:S(2)}, u32[]{:S(2)}) collective-permute-start(s32[]{:T(128)} %get-tuple-element.59), channel_id=1, source_target_pairs={{0,64},{32,96},{64,0},{96,32},{1,65},{33,97},{65,1},{97,33},{2,66}... | collective-permute-start | bytes 20 | tf_op jit(solution)/shard_map/ppermute | solution.py:495
  122.1 21.1 %collective-permute-start.4 = (s32[]{:T(128)}, s32[]{:T(128)}, u32[]{:S(2)}, u32[]{:S(2)}) collective-permute-start(s32[]{:T(128)} %get-tuple-element.59), channel_id=1, source_target_pairs={{0,96},{32,0},{64,32},{96,64},{1,97},{33,1},{65,33},{97,65},{2,98}... | collective-permute-start | bytes 20 | tf_op jit(solution)/shard_map/ppermute | solution.py:495
Sparse Core Ops, SparseCore 0:
  20.9 187.8 all-gather.1
